TPU v7x, 512 devices: a whole 4x4x16 slice. The times are simulated.
512 devices in a mesh: req: 16 (over x, y), ctx: 32 (over z, core).
Axes of the slice: x: 4, y: 4, z: 16, core: 2. Of those that a mesh axis runs over, the one named last changes fastest.
Arguments:
- query: bfloat16 [2048, 4096], P(('req', 'ctx')), may hold values from -8 to 8
- prefix_id: int32 [2048], P('req'), may hold values from 0 to 31, as said below
- suffix_blocks: int32 [512, 4], P(('req', 'ctx')), may hold values from 1 to 2, 6 in all within a row
- prefix_kv: bfloat16 [32, 16384, 1024], P('ctx', 'req'), may hold values from -6 to 6
- suffix_kv: bfloat16 [2048, 256, 1024], P(('req', 'ctx')), may hold values from -8 to 8
- w_out: bfloat16 [4096, 5120], P('ctx', 'req'), may hold values from -0.046875 to 0.046875
Outputs:
- projected: bfloat16 [2048, 5120], P(('req', 'ctx'))
Inputs may be any that keep to these rules, and one draw needn't show every extreme that they name: `prefix_id`: in each aligned block of 128 rows (one request group) the same two ids are named exactly 8 times, every other id at most 4 times, and the 4 rows of some one device all name one id. `suffix_blocks`: the 4 entries of one device sum to 6.
All inputs are finite; a program needn't handle non-finite values.
Results may differ from a plain program's by a relative error of at most 0.005.
Values may be sent and summed in bfloat16 or wider, within the bound.
No kernel may reach another device: no remote copies, remote signals or barrier semaphores. Data moves between devices by JAX's collectives and lax.ppermute only.
A program may use at most 64 MiB of HBM per device.

v0:
```python
import math

import jax
import jax.numpy as jnp
from jax import lax
from jax.sharding import PartitionSpec as P

KVH = 4
HD = 128
SB = 128
G_MAX = 8


NEGATIVE = -1e30
HIGH = lax.Precision.HIGHEST


def attend(queries, key_rows, value_rows, factor):
    scores = (
        lax.dot_general(
            queries, key_rows, (((1,), (1,)), ((), ())), preferred_element_type=jnp.float32
        )
        * factor
    )
    maxima = jnp.max(scores, axis=-1, keepdims=True)
    expo = jnp.exp(scores - maxima)
    summed = jnp.sum(expo, axis=-1, keepdims=True)
    weights = expo.astype(jnp.bfloat16)
    output = jnp.dot(weights, value_rows, preferred_element_type=jnp.float32) / summed
    return (output, maxima[:, 0] + jnp.log(summed[:, 0]))


def owner_attention(gathered, local_block, factor):
    slot_count = gathered.shape[0]
    head_count = gathered.shape[1] // HD
    group_size = head_count // KVH
    key_width = KVH * HD
    key_rows = local_block[:, :key_width].reshape(-1, KVH, HD).transpose(1, 0, 2)
    value_rows = local_block[:, key_width:].reshape(-1, KVH, HD).transpose(1, 0, 2)
    row_count = slot_count * group_size
    tile_rows = math.gcd(row_count, 512)
    queries = gathered.reshape(slot_count, KVH, group_size, HD).transpose(1, 0, 2, 3)
    queries = queries.reshape(KVH, row_count // tile_rows, tile_rows, HD)

    def per_head(operands):
        head_queries, head_keys, head_values = operands

        def per_tile(row_tile):
            return attend(row_tile, head_keys, head_values, factor)

        return lax.map(per_tile, head_queries)

    output, log_total = lax.map(per_head, (queries, key_rows, value_rows))
    output = output.reshape(KVH, slot_count, group_size, HD).transpose(1, 0, 2, 3)
    log_total = log_total.reshape(KVH, slot_count, group_size).transpose(1, 0, 2)
    return (output.reshape(slot_count, head_count * HD), log_total.reshape(slot_count, head_count))


def merge_blocks(outputs, log_totals):
    blocks, slot_count, head_count = log_totals.shape
    peak = jnp.max(log_totals, axis=0)
    factors = jnp.exp(log_totals - peak)
    summed = jnp.sum(factors, axis=0)
    shaped = outputs.reshape(blocks, slot_count, head_count, HD)
    merged = jnp.sum(factors[..., None] * shaped, axis=0) / summed[..., None]
    return (merged.reshape(slot_count, head_count * HD), peak + jnp.log(summed))


def suffix_attention(query, suffix_kv, lengths, factor):
    row_count = query.shape[0]
    head_count = query.shape[1] // HD
    group_size = head_count // KVH
    key_width = KVH * HD
    positions = suffix_kv.shape[1]
    shaped = query.reshape(row_count, KVH, group_size, HD)
    key_rows = suffix_kv[:, :, :key_width].reshape(row_count, positions, KVH, HD)
    value_rows = suffix_kv[:, :, key_width:].reshape(row_count, positions, KVH, HD)
    scores = (
        jnp.einsum("rkgd,rskd->rkgs", shaped, key_rows, preferred_element_type=jnp.float32) * factor
    )
    live = jnp.arange(positions, dtype=jnp.int32)[None, :] < lengths[:, None]
    scores = jnp.where(live[:, None, None, :], scores, NEGATIVE)
    maxima = jnp.max(scores, axis=-1, keepdims=True)
    expo = jnp.exp(scores - maxima)
    summed = jnp.sum(expo, axis=-1, keepdims=True)
    weights = expo.astype(jnp.bfloat16)
    output = (
        jnp.einsum("rkgs,rskd->rkgd", weights, value_rows, preferred_element_type=jnp.float32)
        / summed
    )
    log_total = maxima[..., 0] + jnp.log(summed[..., 0])
    return (output.reshape(row_count, head_count * HD), log_total.reshape(row_count, head_count))


def combine_parts(prefix_out, prefix_log, suffix_out, suffix_log):
    slot_count, head_count = prefix_log.shape
    top_log = jnp.maximum(prefix_log, suffix_log)
    prefix_weight = jnp.exp(prefix_log - top_log)[..., None]
    suffix_weight = jnp.exp(suffix_log - top_log)[..., None]
    mixed = (
        prefix_weight * prefix_out.reshape(slot_count, head_count, HD)
        + suffix_weight * suffix_out.reshape(slot_count, head_count, HD)
    ) / (prefix_weight + suffix_weight)
    return mixed.reshape(slot_count, head_count * HD).astype(jnp.bfloat16)


def local(query, prefix_id, suffix_blocks, prefix_kv, suffix_kv, w_out):
    factor = HD ** (-0.5)
    owner_index = lax.axis_index("ctx")
    req_count = lax.axis_size("req")
    ctx_count = lax.axis_size("ctx")
    row_count = query.shape[0]
    slot_count = G_MAX
    group_queries = lax.all_gather(query, "ctx", axis=0, tiled=True)
    owned_rows = prefix_id == owner_index
    row_rank = jnp.cumsum(owned_rows.astype(jnp.int32)) - 1
    selector = jnp.logical_and(
        owned_rows[None, :], row_rank[None, :] == jnp.arange(slot_count, dtype=jnp.int32)[:, None]
    )
    picked = jnp.dot(
        selector.astype(jnp.bfloat16), group_queries, preferred_element_type=jnp.float32
    ).astype(jnp.bfloat16)
    gathered = lax.all_gather(picked, "req", axis=0, tiled=True)
    block_out, block_log = owner_attention(gathered, prefix_kv[0], factor)
    received_out, received_log = (
        lax.all_to_all(
            block_out.reshape(req_count, slot_count, -1),
            "req",
            split_axis=0,
            concat_axis=0,
            tiled=True,
        ),
        lax.all_to_all(
            block_log.reshape(req_count, slot_count, -1),
            "req",
            split_axis=0,
            concat_axis=0,
            tiled=True,
        ),
    )
    prefix_out, prefix_log = merge_blocks(received_out, received_log)
    suffix_out, suffix_log = suffix_attention(query, suffix_kv, suffix_blocks[0] * SB, factor)
    placing = selector.astype(jnp.float32).T
    spread_out = jnp.dot(placing, prefix_out, precision=HIGH, preferred_element_type=jnp.float32)
    spread_log = jnp.dot(placing, prefix_log, precision=HIGH, preferred_element_type=jnp.float32)
    home_out, home_log = (
        lax.all_to_all(
            spread_out.reshape(ctx_count, row_count, -1),
            "ctx",
            split_axis=0,
            concat_axis=0,
            tiled=True,
        ),
        lax.all_to_all(
            spread_log.reshape(ctx_count, row_count, -1),
            "ctx",
            split_axis=0,
            concat_axis=0,
            tiled=True,
        ),
    )
    attention = combine_parts(
        jnp.sum(home_out, axis=0), jnp.sum(home_log, axis=0), suffix_out, suffix_log
    )
    head_rows = lax.all_to_all(attention, "ctx", split_axis=1, concat_axis=0, tiled=True)
    terms = jnp.dot(
        head_rows,
        lax.all_gather(w_out, "req", axis=1, tiled=True),
        preferred_element_type=jnp.float32,
    )
    summed = lax.psum_scatter(terms, "ctx", scatter_dimension=0, tiled=True)
    return summed.astype(jnp.bfloat16)


def solution(mesh):
    in_specs = (
        P(("req", "ctx"), None),
        P("req"),
        P(("req", "ctx"), None),
        P("ctx", "req", None),
        P(("req", "ctx"), None, None),
        P("ctx", "req"),
    )
    out_specs = P(("req", "ctx"), None)
    return jax.shard_map(local, mesh=mesh, in_specs=in_specs, out_specs=out_specs, check_vma=False)
```

profile of v0, /device:TPU:1, one launch (start us, length us, event | category | flops | bytes accessed | tf_op | source)
XLA Modules:
  0.0 484.2 jit_solution(13851486390008122569)
XLA Ops:
  8.4 77.5 %all-gather.9.cloned.1.call-done = bf16[32,4,4096]{2,1,0:T(4,128)(2,1)} async-done(((bf16[1,4,4096]{2,1,0:T(4,128)(2,1)}), bf16[32,4,4096]{2,1,0:T(4,128)(2,1)}) %all-gather.9.cloned.1.call-update) | async-done | bytes 1048592 | tf_op jit(solution)/shard_map/all_gather | solution.py:114
  88.1 2.9 copy.33
  92.5 49.8 %all-gather.5.cloned.1.call-done = bf16[128,4096]{1,0:T(8,128)(2,1)} async-done(((bf16[8,4096]{1,0:T(8,128)(2,1)}), bf16[128,4096]{1,0:T(8,128)(2,1)}) %all-gather.5.cloned.1.call-update) | async-done | bytes 1048592 | tf_op jit(solution)/shard_map/all_gather | solution.py:123
  144.9 26.1 %while.25 = (s32[]{:T(128)}, f32[4,2,512,128]{3,2,1,0:T(8,128)}, f32[4,2,512]{2,1,0:T(2,128)S(1)}, bf16[4,2,512,128]{3,2,1,0:T(8,128)(2,1)}, bf16[4,1024,128]{1,...) while((s32[]{:T(128)}, f32[4,2,512,128]{3,2,1,0:T(8,128)}, ...), condition=%wide.region_6.7_spmd, body=%wide.region_1.6_spmd.sunk | while | flops 272694784 | bytes 10908442 | solution.py:53
  147.3 3.2 while.26
  153.8 3.2 while.26
  160.3 3.2 while.26
  166.9 3.2 while.26
  172.2 5.0 %all-to-all-start = ((f32[16,1,256]{2,1,0:T(1,128)}), f32[16,1,256]{2,1,0:T(1,128)S(1)}, u32[]{:S(2)}, u32[]{:S(2)}) async-start(f32[16,1,256]{2,1,0:T(1,128)} %reshape.210), calls=%async_computation | async-start | bytes 32768 | tf_op jit(solution)/shard_map/all_to_all | solution.py:133
  177.2 1.9 copy.76
  179.0 1.6 reshape_reshape.10
  180.6 3.0 all-to-all-done
  183.6 3.7 all-to-all-start.2
  190.1 22.4 %all-to-all-done.2 = f32[16,8,4096]{2,1,0:T(8,128)S(1)} async-done(((f32[16,8,4096]{2,1,0:T(8,128)}), f32[16,8,4096]{2,1,0:T(8,128)S(1)}, u32[]{:S(2)}, u32[]{:S(2)}) %all-to-all-start.2) | async-done | bytes 2097184 | tf_op jit(solution)/shard_map/all_to_all | solution.py:126
  212.6 18.0 %all-to-all-start.1 = ((f32[32,1,128]{2,1,0:T(1,128)}), f32[32,1,128]{2,1,0:T(1,128)S(1)}, u32[]{:S(2)}, u32[]{:S(2)}) async-start(f32[32,1,128]{2,1,0:T(1,128)} %reshape.212), calls=%async_computation.1 | async-start | bytes 32768 | tf_op jit(solution)/shard_map/all_to_all | solution.py:154
  232.4 2.7 copy.47
  235.1 7.2 %all-to-all-done.1 = f32[32,1,128]{2,1,0:T(1,128)S(1)} async-done(((f32[32,1,128]{2,1,0:T(1,128)}), f32[32,1,128]{2,1,0:T(1,128)S(1)}, u32[]{:S(2)}, u32[]{:S(2)}) %all-to-all-start.1) | async-done | bytes 16416 | tf_op jit(solution)/shard_map/all_to_all | solution.py:154
  242.3 5.0 %all-to-all-start.3 = ((f32[32,4,4096]{2,1,0:T(4,128)}), f32[32,4,4096]{2,1,0:T(4,128)S(1)}, u32[]{:S(2)}, u32[]{:S(2)}) async-start(f32[32,4,4096]{2,1,0:T(4,128)} %copy.47), calls=%async_computation.3 | async-start | bytes 4194304 | tf_op jit(solution)/shard_map/all_to_all | solution.py:147
  248.0 3.0 fusion.49
  256.2 89.7 %all-to-all-done.3 = f32[32,4,4096]{2,1,0:T(4,128)S(1)} async-done(((f32[32,4,4096]{2,1,0:T(4,128)}), f32[32,4,4096]{2,1,0:T(4,128)S(1)}, u32[]{:S(2)}, u32[]{:S(2)}) %all-to-all-start.3) | async-done | bytes 2097184 | tf_op jit(solution)/shard_map/all_to_all | solution.py:147
  347.0 5.2 %all-to-all-start.4 = ((bf16[4,32,128]{2,0,1:T(4,128)(2,1)}), bf16[4,32,128]{2,0,1:T(4,128)(2,1)S(1)}, u32[]{:S(2)}, u32[]{:S(2)}) async-start(bf16[4,32,128]{2,0,1:T(4,128)(2,1)} %fusion.24), calls=%async_computation.4 | async-start | bytes 65536 | tf_op jit(solution)/shard_map/all_to_all | solution.py:165
  354.2 10.0 %all-to-all-done.4 = bf16[4,32,128]{2,0,1:T(4,128)(2,1)S(1)} async-done(((bf16[4,32,128]{2,0,1:T(4,128)(2,1)}), bf16[4,32,128]{2,0,1:T(4,128)(2,1)S(1)}, u32[]{:S(2)}, u32[]{:S(2)}) %all-to-all-start.4) | async-done | bytes 32800 | tf_op jit(solution)/shard_map/all_to_all | solution.py:165
  364.3 1.8 fusion.51
  366.1 110.0 %all-reduce.2 = bf16[128,5120]{1,0:T(8,128)(2,1)} all-reduce(f32[128,5120]{1,0:T(8,128)S(1)} %fusion.51), channel_id=2, replica_groups=mesh['req'=16,'ctx'=32] {'ctx'}, use_global_device_ids=true, to_apply=%region_14.15.clone | all-reduce | flops 655360 | bytes 3932160
  (133 shorter events, 49.4 us)
Async XLA Ops:
  6.5 79.3 %all-gather.9.cloned.1.call-start = ((), (), s32[]{:S(2)}) async-start(), calls=%async_computation.7 | async-start | bytes 1081344 | tf_op jit(solution)/shard_map/all_gather | solution.py:114
  7.3 135.0 %all-gather.5.cloned.1.call-start = ((), (), s32[]{:S(2)}) async-start(), calls=%async_computation.5 | async-start | bytes 1114112 | tf_op jit(solution)/shard_map/all_gather | solution.py:123
  172.2 11.4 %all-to-all-start = ((f32[16,1,256]{2,1,0:T(1,128)}), f32[16,1,256]{2,1,0:T(1,128)S(1)}, u32[]{:S(2)}, u32[]{:S(2)}) async-start(f32[16,1,256]{2,1,0:T(1,128)} %reshape.210), calls=%async_computation | async-start | bytes 32768 | tf_op jit(solution)/shard_map/all_to_all | solution.py:133
  183.6 29.0 %all-to-all-start.2 = ((f32[16,8,4096]{2,1,0:T(8,128)}), f32[16,8,4096]{2,1,0:T(8,128)S(1)}, u32[]{:S(2)}, u32[]{:S(2)}) async-start(f32[16,8,4096]{2,1,0:T(8,128)} %reshape_reshape.10), calls=%async_computation.2 | async-start | bytes 4194304 | tf_op jit(solution)/shard_map/all_to_all | solution.py:126
  212.6 29.7 %all-to-all-start.1 = ((f32[32,1,128]{2,1,0:T(1,128)}), f32[32,1,128]{2,1,0:T(1,128)S(1)}, u32[]{:S(2)}, u32[]{:S(2)}) async-start(f32[32,1,128]{2,1,0:T(1,128)} %reshape.212), calls=%async_computation.1 | async-start | bytes 32768 | tf_op jit(solution)/shard_map/all_to_all | solution.py:154
  242.3 103.6 %all-to-all-start.3 = ((f32[32,4,4096]{2,1,0:T(4,128)}), f32[32,4,4096]{2,1,0:T(4,128)S(1)}, u32[]{:S(2)}, u32[]{:S(2)}) async-start(f32[32,4,4096]{2,1,0:T(4,128)} %copy.47), calls=%async_computation.3 | async-start | bytes 4194304 | tf_op jit(solution)/shard_map/all_to_all | solution.py:147
  247.3 107.0 %all-gather.7.cloned.1.call-start = ((), (), s32[]{:S(2)}) async-start(), calls=%async_computation.6 | async-start | bytes 1392640 | tf_op jit(solution)/shard_map/all_gather | solution.py:168
  251.0 1.5 copy-start.1
  251.0 1.6 copy-start
  347.0 17.3 %all-to-all-start.4 = ((bf16[4,32,128]{2,0,1:T(4,128)(2,1)}), bf16[4,32,128]{2,0,1:T(4,128)(2,1)S(1)}, u32[]{:S(2)}, u32[]{:S(2)}) async-start(bf16[4,32,128]{2,0,1:T(4,128)(2,1)} %fusion.24), calls=%async_computation.4 | async-start | bytes 65536 | tf_op jit(solution)/shard_map/all_to_all | solution.py:165
Sparse Core Ops, SparseCore 0:
  9.5 76.3 all-gather.8
  88.9 53.3 all-gather.4
  251.2 55.7 all-gather.6
where the time goes:
time: 486 us; the launch traced here: 484 us
  waiting for transfers between devices  261 us (54%)
  blocking collectives  110 us (23%)
  local copies, waits for them, and re-layouts  40.2 us (8%)
  starting transfers between devices  36.9 us (8%)
  between operations  14.1 us (3%)
  matrix products  13.1 us (3%)
  other arithmetic  8.5 us (2%)
    unnamed x1, blocking collectives  110 us
    all_to_all x1, waiting for transfers between devices, local(): lax.all_to_all(spread_out.reshape(ctx_count, row_count, -1), 'ctx', split...  89.7 us
    all_gather x1, waiting for transfers between devices, local(): group_queries = lax.all_gather(query, 'ctx', axis=0, tiled=True)  77.5 us
    all_gather x1, waiting for transfers between devices, local(): gathered = lax.all_gather(picked, 'req', axis=0, tiled=True)  49.8 us
    all_to_all x1, waiting for transfers between devices, local(): lax.all_to_all(block_out.reshape(req_count, slot_count, -1), 'req', split...  22.4 us
    all_to_all x1, starting transfers between devices, local(): lax.all_to_all(spread_log.reshape(ctx_count, row_count, -1), 'ctx', split...  18 us
    unnamed x14, local copies, waits for them, and re-layouts  11.6 us
    all_to_all x1, waiting for transfers between devices, local(): lax.all_to_all(attention, 'ctx', split_axis=1, concat_axis=0, tiled=True)  10 us
  transfers between devices with their start and end apart: 8, of which 7 were waited for; matrix products, arithmetic and copies ran while one was open for 6% of the time, Pallas kernels for 0%

commit v1 on v0

v1 whole, which is shorter than its diff:
```python
import functools

import jax
import jax.numpy as jnp
from jax import lax
from jax.experimental import pallas as pl
from jax.experimental.pallas import tpu as pltpu
from jax.sharding import PartitionSpec as P

KVH = 4
HD = 128
SB = 128
SLOTS = 8
GROUP = 8
FACTOR = HD**-0.5
LOG2E = 1.4426950408889634
NEGATIVE = -1e30
BF16 = jnp.bfloat16
F32 = jnp.float32


def split3(x):
    high = lax.reduce_precision(x, 8, 7)
    rest = x - high
    middle = lax.reduce_precision(rest, 8, 7)
    return high.astype(BF16), middle.astype(BF16), (rest - middle).astype(BF16)


def attention_kernel(q_ref, k_ref, v_ref, out_ref, parts_ref):
    head = pl.program_id(0)
    groups, rows, _ = q_ref.shape
    total = groups * rows
    tile = min(256, total)
    keys = k_ref[...]
    values = v_ref[...].T
    queries = q_ref[...].reshape(total, HD)

    @pl.when(head == 0)
    def _():
        parts_ref[...] = jnp.zeros_like(parts_ref)

    per = tile // rows
    for at in range(total // tile):
        scores = lax.dot_general(
            keys, queries[at * tile : (at + 1) * tile], (((1,), (1,)), ((), ())),
            preferred_element_type=F32,
        )
        top = jnp.max(scores, axis=0, keepdims=True)
        expo = jnp.exp2((scores - top) * (FACTOR * LOG2E))
        summed = jnp.sum(expo, axis=0, keepdims=True)
        output = jnp.dot(values, expo.astype(BF16), preferred_element_type=F32) / summed
        out_ref[at * per : (at + 1) * per, pl.ds(pl.multiple_of(head * rows, rows), rows), :] = (
            output.T.astype(BF16).reshape(per, rows, HD)
        )
        lse = top * FACTOR + jnp.log(summed)
        high = lse.astype(BF16).astype(F32)
        rest = lse - high
        middle = rest.astype(BF16).astype(F32)
        cols = slice(at * tile, (at + 1) * tile)
        parts_ref[pl.ds(head, 1), cols] = high
        parts_ref[pl.ds(KVH + head, 1), cols] = middle
        parts_ref[pl.ds(2 * KVH + head, 1), cols] = rest - middle

    @pl.when(head == KVH - 1)
    def _():
        whole = parts_ref[...]
        rolled = pltpu.roll(whole, total - rows, 1)
        for r in range(groups):
            source = whole if r % 2 == 0 else rolled
            at = r // 2 * 128
            out_ref[r, KVH * rows :, :] = source[:, at : at + 128].astype(BF16)


def prefix_attention(queries, kv):
    groups, rows, _ = queries.shape
    tokens = kv.shape[0]
    each = rows // KVH
    return pl.pallas_call(
        attention_kernel,
        out_shape=jax.ShapeDtypeStruct((groups, rows + 16, HD), BF16),
        grid=(KVH,),
        in_specs=[
            pl.BlockSpec((groups, each, HD), lambda h: (0, h, 0)),
            pl.BlockSpec((tokens, HD), lambda h: (0, h)),
            pl.BlockSpec((tokens, HD), lambda h: (0, KVH + h)),
        ],
        out_specs=pl.BlockSpec((groups, rows + 16, HD), lambda h: (0, 0, 0)),
        scratch_shapes=[pltpu.VMEM((16, groups * each), F32)],
        compiler_params=pltpu.CompilerParams(vmem_limit_bytes=48 * 2**20),
        cost_estimate=pl.CostEstimate(
            flops=4 * groups * rows * tokens * HD,
            bytes_accessed=4 * groups * rows * HD + 4 * tokens * KVH * HD,
            transcendentals=groups * rows * tokens,
        ),
    )(queries, kv, kv)


def suffix_attention(query, suffix_kv, lengths):
    rows = query.shape[0]
    positions = suffix_kv.shape[1]
    shaped = query.reshape(rows, KVH, -1, HD)
    keys = suffix_kv[:, :, : KVH * HD].reshape(rows, positions, KVH, HD)
    values = suffix_kv[:, :, KVH * HD :].reshape(rows, positions, KVH, HD)
    scores = jnp.einsum("rkgd,rskd->rkgs", shaped, keys, preferred_element_type=F32) * FACTOR
    live = jnp.arange(positions, dtype=jnp.int32)[None, :] < lengths[:, None]
    scores = jnp.where(live[:, None, None, :], scores, NEGATIVE)
    top = jnp.max(scores, axis=-1, keepdims=True)
    expo = jnp.exp(scores - top)
    summed = jnp.sum(expo, axis=-1, keepdims=True)
    output = (
        jnp.einsum("rkgs,rskd->rkgd", expo.astype(BF16), values, preferred_element_type=F32)
        / summed
    )
    lse = top + jnp.log(summed)
    return output.reshape(rows, -1, HD), lse.reshape(rows, -1, 1)


def a2a(x, axis, groups=None):
    return lax.all_to_all(x, axis, 0, 0, tiled=True, axis_index_groups=groups)


def local(query, prefix_id, suffix_blocks, prefix_kv, suffix_kv, w_out):
    req = lax.axis_size("req")
    ctx = lax.axis_size("ctx")
    rows = query.shape[0]
    heads = query.shape[1] // HD
    group_rows = rows * ctx
    slots = ctx * SLOTS
    near = [list(range(a, a + GROUP)) for a in range(0, ctx, GROUP)]
    width = w_out.shape[1] // GROUP

    with jax.named_scope("weights"):
        block = w_out.T.reshape(GROUP, width, HD)
        block = a2a(block, "ctx", near).transpose(1, 0, 2).reshape(width, GROUP * HD)
        weights = lax.all_gather(block, "req", axis=0, tiled=True)

    with jax.named_scope("suffix"):
        suffix_out, suffix_lse = suffix_attention(query, suffix_kv, suffix_blocks[0] * SB)

    with jax.named_scope("query_to_heads"):
        payload = jnp.concatenate(
            [
                query.reshape(rows, heads, HD),
                suffix_out.astype(BF16),
                *split3(suffix_lse),
                jnp.zeros((rows, heads, HD - 3), BF16),
            ],
            axis=-1,
        )
        by_head = a2a(payload.transpose(1, 0, 2), "ctx").reshape(group_rows, 3 * HD)

    with jax.named_scope("heads_to_slots"):
        index = jnp.arange(group_rows, dtype=jnp.int32)
        same = prefix_id[:, None] == prefix_id[None, :]
        rank = jnp.sum((same & (index[None, :] < index[:, None])).astype(jnp.int32), axis=1)
        slot = prefix_id * SLOTS + rank
        place = (slot[None, :] == jnp.arange(slots, dtype=jnp.int32)[:, None]).astype(BF16)
        picked = jnp.dot(place, by_head[:, :HD], preferred_element_type=F32).astype(BF16)
        by_slot = a2a(picked.reshape(ctx, SLOTS, HD), "ctx").reshape(heads * SLOTS, HD)

    with jax.named_scope("gather_req"):
        spread = jnp.broadcast_to(by_slot[None], (req, *by_slot.shape))
        gathered = a2a(spread, "req")

    with jax.named_scope("prefix"):
        partials = prefix_attention(gathered, prefix_kv[0])
        received = a2a(partials, "req")

    with jax.named_scope("merge"):
        count = heads * SLOTS
        logs = received[:, count : count + 3 * KVH, : count // KVH].astype(F32)
        logs = jnp.sum(logs.reshape(req, 3, count), axis=1)
        peak = jnp.max(logs, axis=0)
        shares = jnp.exp(logs - peak)
        total = jnp.sum(shares, axis=0)
        merged = jnp.sum(shares[..., None] * received[:, :count].astype(F32), axis=0)
        merged = (merged / total[:, None]).astype(BF16)
        merged_lse = (peak + jnp.log(total))[:, None]

    with jax.named_scope("slots_to_heads"):
        payload = jnp.concatenate(
            [merged, *split3(merged_lse), jnp.zeros((count, HD - 3), BF16)], axis=-1
        )
        arrived = a2a(payload.reshape(heads, SLOTS, 2 * HD), "ctx").reshape(slots, 2 * HD)

    with jax.named_scope("mix"):
        prefix = lax.dot_general(
            place, arrived, (((0,), (0,)), ((), ())), preferred_element_type=F32
        )
        prefix_lse = jnp.sum(prefix[:, HD : HD + 3], axis=1, keepdims=True)
        own = by_head[:, HD:].astype(F32)
        own_lse = jnp.sum(own[:, HD : HD + 3], axis=1, keepdims=True)
        top = jnp.maximum(prefix_lse, own_lse)
        prefix_share = jnp.exp(prefix_lse - top)
        own_share = jnp.exp(own_lse - top)
        attention = (prefix_share * prefix[:, :HD] + own_share * own[:, :HD]) / (
            prefix_share + own_share
        )
        attention = attention.astype(BF16)

    with jax.named_scope("projection"):
        shared = a2a(jnp.broadcast_to(attention[None], (GROUP, *attention.shape)), "ctx", near)
        shared = shared.transpose(1, 0, 2).reshape(group_rows, GROUP * HD)
        terms = lax.dot_general(
            shared, weights, (((1,), (1,)), ((), ())), preferred_element_type=F32
        ).astype(BF16)
        home = a2a(terms.reshape(ctx, rows, -1), "ctx")
        home = home.reshape(ctx // GROUP, GROUP, rows, req, width).astype(F32)
        summed = jnp.sum(home, axis=0).transpose(1, 2, 0, 3)
        return summed.reshape(rows, -1).astype(BF16)


def solution(mesh):
    in_specs = (
        P(("req", "ctx"), None),
        P("req"),
        P(("req", "ctx"), None),
        P("ctx", "req", None),
        P(("req", "ctx"), None, None),
        P("ctx", "req"),
    )
    out_specs = P(("req", "ctx"), None)
    return jax.shard_map(local, mesh=mesh, in_specs=in_specs, out_specs=out_specs, check_vma=False)
```

time: 486 us -> 206 us (0.42)
  waiting for transfers between devices: 261 us -> 56.5 us
  blocking collectives: 110 us -> 67.4 us
  local copies, waits for them, and re-layouts: 40.2 us -> 9.55 us
  Pallas kernels: 0 us -> 14.2 us
  matrix products: 13.1 us -> 2.98 us
  other arithmetic: 8.5 us -> 1.88 us
    all_gather x3 -> x1, waiting for transfers between devices: 127 us -> 6.58 us  [local(): weights = lax.all_gather(block, 'req', axis=0, tiled=True)]
    unnamed x1 -> x0, blocking collectives: 110 us -> none
    all_to_all x5, waiting for transfers between devices: 132 us -> 49.9 us  [a2a(): return lax.all_to_all(x, axis, 0, 0, tiled=True, axis_index_groups=groups)]
    all_to_all x0 -> x3, blocking collectives: none -> 67.4 us  [a2a(): return lax.all_to_all(x, axis, 0, 0, tiled=True, axis_index_groups=groups)]
    pallas_call x0 -> x1, Pallas kernels: none -> 14.2 us  [prefix_attention(): pl.pallas_call(attention_kernel, out_shape=jax.ShapeDtypeStruct((groups,...]
    unnamed x14 -> x10, local copies, waits for them, and re-layouts: 11.6 us -> 1.32 us
    dot_general x22 -> x5, matrix products: 13.1 us -> 2.98 us  [the longest x1 1.86 us: local(): lax.dot_general(shared, weights, (((1,), (1,)), ((), ())), preferred_elem...]
    dynamic_slice x12 -> x0, local copies, waits for them, and re-layouts: 5.62 us -> none  [owner_attention(): output, log_total = lax.map(per_head, (queries, key_rows, value_rows))]
  transfers between devices with their start and end apart: 8 -> 6, of which waited for: 7 -> 5; matrix products, arithmetic and copies ran while one was open for 6% -> 2% of each run, Pallas kernels for 0% -> 7%
where the time goes in v1:
time: 206 us; the launch traced here: 205 us
  blocking collectives  67.4 us (33%)
  waiting for transfers between devices  56.5 us (27%)
  starting transfers between devices  39 us (19%)
  Pallas kernels  14.2 us (7%)
  between operations  13.6 us (7%)
  local copies, waits for them, and re-layouts  9.55 us (5%)
  matrix products  2.98 us (1%)
    all_to_all x3, blocking collectives, a2a(): return lax.all_to_all(x, axis, 0, 0, tiled=True, axis_index_groups=groups)  67.4 us
    all_to_all x5, waiting for transfers between devices, a2a(): return lax.all_to_all(x, axis, 0, 0, tiled=True, axis_index_groups=groups)  49.9 us
    all_to_all x5, starting transfers between devices, a2a(): return lax.all_to_all(x, axis, 0, 0, tiled=True, axis_index_groups=groups)  38.9 us
    pallas_call x1, Pallas kernels, prefix_attention(): pl.pallas_call(attention_kernel, out_shape=jax.ShapeDtypeStruct((groups,...  14.2 us
    all_gather x1, waiting for transfers between devices, local(): weights = lax.all_gather(block, 'req', axis=0, tiled=True)  6.58 us
  transfers between devices with their start and end apart: 6, of which 5 were waited for; matrix products, arithmetic and copies ran while one was open for 2% of the time, Pallas kernels for 7%

profile of v1, /device:TPU:1, one launch (start us, length us, event | category | flops | bytes accessed | tf_op | source)
XLA Modules:
  0.0 205.1 jit_solution(4158858286419128600)
XLA Ops:
  6.5 1.8 fusion.28
  8.3 0.5 copy.83
  11.2 0.9 concatenate.7
  12.1 16.7 %all-to-all-start = ((bf16[32,4,384]{2,1,0:T(4,128)(2,1)}), bf16[32,4,384]{2,1,0:T(4,128)(2,1)S(1)}, u32[]{:S(2)}, u32[]{:S(2)}) async-start(bf16[32,4,384]{2,1,0:T(4,128)(2,1)} %bitcast.5), calls=%async_computation | async-start | bytes 196608 | tf_op jit(solution)/shard_map/query_to_heads/all_to_all | solution.py:119
  29.0 14.4 %all-to-all-done = bf16[32,4,384]{2,1,0:T(4,128)(2,1)S(1)} async-done(((bf16[32,4,384]{2,1,0:T(4,128)(2,1)}), bf16[32,4,384]{2,1,0:T(4,128)(2,1)S(1)}, u32[]{:S(2)}, u32[]{:S(2)}) %all-to-all-start) | async-done | bytes 98336 | tf_op jit(solution)/shard_map/query_to_heads/all_to_all | solution.py:119
  43.6 17.1 %all_to_all.40 = bf16[32,8,128]{2,1,0:T(8,128)(2,1)S(1)} all-to-all(bf16[32,8,128]{2,1,0:T(8,128)(2,1)S(1)} %fusion.1), channel_id=1, replica_groups=mesh['req'=16,'ctx'=32] {'ctx'}, dimensions={0} | all-to-all | bytes 131072 | tf_op jit(solution)/shard_map/heads_to_slots/all_to_all | solution.py:119
  61.0 21.6 %all_to_all.41.q_ref = bf16[16,256,128]{2,1,0:T(8,128)(2,1)S(1)} all-to-all(bf16[16,256,128]{2,1,0:T(8,128)(2,1)S(1)} %broadcast_in_dim.26), channel_id=1, replica_groups=mesh['req'=16,'ctx'=32] {'req'}, dimensions={0} | all-to-all | bytes 2097152 | tf_op jit(solution)/shard_map/gather_req/all_to_all | solution.py:119
  82.6 6.4 %all-to-all-start.6 = ((bf16[8,40,128]{2,1,0:T(8,128)(2,1)}), bf16[8,40,128]{2,1,0:T(8,128)(2,1)S(1)}, u32[]{:S(2)}, u32[]{:S(2)}) async-start(bf16[8,40,128]{2,1,0:T(8,128)(2,1)} %bitcast.14), calls=%async_computation.6 | async-start | bytes 163840 | tf_op jit(solution)/shard_map/weights/all_to_all | solution.py:119
  89.0 14.2 %prefix.1 = bf16[16,272,128]{2,1,0:T(8,128)(2,1)} custom-call(bf16[16,256,128]{2,1,0:T(8,128)(2,1)S(1)} %all_to_all.41.q_ref, bf16[1024,1024]{1,0:T(8,128)(2,1)S(1)} %bitcast.48, bf16[1024,1024]{1,0:T(8,128)(2,1)S(1)} %bitcast.49), custom_call_target="tpu_custom_call" | custom-call | flops 2147483648 | bytes 4194304 | tf_op jit(solution)/shard_map/prefix/pallas_call | solution.py:78
  103.2 3.7 %all-to-all-start.3 = ((bf16[16,272,128]{2,1,0:T(8,128)(2,1)}), bf16[16,272,128]{2,1,0:T(8,128)(2,1)S(1)}, u32[]{:S(2)}, u32[]{:S(2)}) async-start(bf16[16,272,128]{2,1,0:T(8,128)(2,1)} %prefix.1), calls=%async_computation.3 | async-start | bytes 2228224 | tf_op jit(solution)/shard_map/prefix/all_to_all | solution.py:119
  106.9 0.6 copy_bitcast_fusion
  107.6 17.6 %all-to-all-done.3 = bf16[16,272,128]{2,1,0:T(8,128)(2,1)S(1)} async-done(((bf16[16,272,128]{2,1,0:T(8,128)(2,1)}), bf16[16,272,128]{2,1,0:T(8,128)(2,1)S(1)}, u32[]{:S(2)}, u32[]{:S(2)}) %all-to-all-start.3) | async-done | bytes 1114144 | tf_op jit(solution)/shard_map/prefix/all_to_all | solution.py:119
  125.7 0.7 multiply_reduce_fusion
  127.1 0.8 concatenate.8
  127.9 7.2 %all-to-all-start.4 = ((bf16[32,8,256]{2,1,0:T(8,128)(2,1)}), bf16[32,8,256]{2,1,0:T(8,128)(2,1)S(1)}, u32[]{:S(2)}, u32[]{:S(2)}) async-start(bf16[32,8,256]{2,1,0:T(8,128)(2,1)} %concatenate.8), calls=%async_computation.4 | async-start | bytes 262144 | tf_op jit(solution)/shard_map/slots_to_heads/all_to_all | solution.py:119
  135.2 15.7 %all-to-all-done.4 = bf16[32,8,256]{2,1,0:T(8,128)(2,1)S(1)} async-done(((bf16[32,8,256]{2,1,0:T(8,128)(2,1)}), bf16[32,8,256]{2,1,0:T(8,128)(2,1)S(1)}, u32[]{:S(2)}, u32[]{:S(2)}) %all-to-all-start.4) | async-done | bytes 131104 | tf_op jit(solution)/shard_map/slots_to_heads/all_to_all | solution.py:119
  151.5 0.8 broadcast_in_dim.28
  152.2 4.9 %all-to-all-start.5 = ((bf16[8,128,128]{1,2,0:T(8,128)(2,1)}), bf16[8,128,128]{1,2,0:T(8,128)(2,1)S(1)}, u32[]{:S(2)}, u32[]{:S(2)}) async-start(bf16[8,128,128]{1,2,0:T(8,128)(2,1)} %broadcast_in_dim.28), calls=%async_computation.5 | async-start | bytes 524288 | tf_op jit(solution)/shard_map/projection/all_to_all | solution.py:119
  157.2 6.6 %all-gather.2.cloned.1.call-done = bf16[640,1024]{1,0:T(8,128)(2,1)} async-done(((bf16[40,1024]{1,0:T(8,128)(2,1)}), bf16[640,1024]{1,0:T(8,128)(2,1)}) %all-gather.2.cloned.1.call-update) | async-done | bytes 1310736 | tf_op jit(solution)/shard_map/weights/all_gather | solution.py:135
  163.7 2.1 %all-to-all-done.5 = bf16[8,128,128]{1,2,0:T(8,128)(2,1)S(1)} async-done(((bf16[8,128,128]{1,2,0:T(8,128)(2,1)}), bf16[8,128,128]{1,2,0:T(8,128)(2,1)S(1)}, u32[]{:S(2)}, u32[]{:S(2)}) %all-to-all-start.5) | async-done | bytes 262176 | tf_op jit(solution)/shard_map/projection/all_to_all | solution.py:119
  165.9 1.9 convolution_convert_fusion
  167.8 28.7 %all_to_all.42 = bf16[32,4,640]{2,1,0:T(4,128)(2,1)S(1)} all-to-all(bf16[32,4,640]{2,1,0:T(4,128)(2,1)S(1)} %reshape.295), channel_id=1, replica_groups=mesh['req'=16,'ctx'=32] {'ctx'}, dimensions={0} | all-to-all | bytes 327680 | tf_op jit(solution)/shard_map/projection/all_to_all | solution.py:119
  196.5 0.8 convert_element_type.133
  197.5 0.8 convert_element_type.137
  (55 shorter events, 5.0 us)
Async XLA Ops:
  8.3 0.7 copy-start.2
  9.0 0.8 copy-start.1
  10.0 18.8 %copy-start.3 = (s32[128]{0:T(128)S(1)}, s32[128]{0:T(128)}, u32[]{:S(2)}) copy-start(s32[128]{0:T(128)} %param.7) | copy-start | bytes 1540
  12.1 31.4 %all-to-all-start = ((bf16[32,4,384]{2,1,0:T(4,128)(2,1)}), bf16[32,4,384]{2,1,0:T(4,128)(2,1)S(1)}, u32[]{:S(2)}, u32[]{:S(2)}) async-start(bf16[32,4,384]{2,1,0:T(4,128)(2,1)} %bitcast.5), calls=%async_computation | async-start | bytes 196608 | tf_op jit(solution)/shard_map/query_to_heads/all_to_all | solution.py:119
  61.0 28.0 %copy-start = (bf16[1,1024,1024]{2,1,0:T(8,128)(2,1)S(1)}, bf16[1,1024,1024]{2,1,0:T(8,128)(2,1)}, u32[]{:S(2)}) copy-start(bf16[1,1024,1024]{2,1,0:T(8,128)(2,1)} %param.9) | copy-start | bytes 6291460
  82.6 20.6 %all-to-all-start.6 = ((bf16[8,40,128]{2,1,0:T(8,128)(2,1)}), bf16[8,40,128]{2,1,0:T(8,128)(2,1)S(1)}, u32[]{:S(2)}, u32[]{:S(2)}) async-start(bf16[8,40,128]{2,1,0:T(8,128)(2,1)} %bitcast.14), calls=%async_computation.6 | async-start | bytes 163840 | tf_op jit(solution)/shard_map/weights/all_to_all | solution.py:119
  103.2 22.1 %all-to-all-start.3 = ((bf16[16,272,128]{2,1,0:T(8,128)(2,1)}), bf16[16,272,128]{2,1,0:T(8,128)(2,1)S(1)}, u32[]{:S(2)}, u32[]{:S(2)}) async-start(bf16[16,272,128]{2,1,0:T(8,128)(2,1)} %prefix.1), calls=%async_computation.3 | async-start | bytes 2228224 | tf_op jit(solution)/shard_map/prefix/all_to_all | solution.py:119
  106.9 56.9 %all-gather.2.cloned.1.call-start = ((), (), s32[]{:S(2)}) async-start(), calls=%async_computation.8 | async-start | bytes 1392640 | tf_op jit(solution)/shard_map/weights/all_gather | solution.py:135
  127.9 23.0 %all-to-all-start.4 = ((bf16[32,8,256]{2,1,0:T(8,128)(2,1)}), bf16[32,8,256]{2,1,0:T(8,128)(2,1)S(1)}, u32[]{:S(2)}, u32[]{:S(2)}) async-start(bf16[32,8,256]{2,1,0:T(8,128)(2,1)} %concatenate.8), calls=%async_computation.4 | async-start | bytes 262144 | tf_op jit(solution)/shard_map/slots_to_heads/all_to_all | solution.py:119
  152.2 13.6 %all-to-all-start.5 = ((bf16[8,128,128]{1,2,0:T(8,128)(2,1)}), bf16[8,128,128]{1,2,0:T(8,128)(2,1)S(1)}, u32[]{:S(2)}, u32[]{:S(2)}) async-start(bf16[8,128,128]{1,2,0:T(8,128)(2,1)} %broadcast_in_dim.28), calls=%async_computation.5 | async-start | bytes 524288 | tf_op jit(solution)/shard_map/projection/all_to_all | solution.py:119
Sparse Core Ops, SparseCore 0:
  110.8 52.9 all-gather.1

commit v2 on v1

v2 whole, which is shorter than its diff:
```python
import functools

import jax
import jax.numpy as jnp
from jax import lax
from jax.experimental import pallas as pl
from jax.experimental.pallas import tpu as pltpu
from jax.sharding import PartitionSpec as P

KVH = 4
HD = 128
SB = 128
SLOTS = 8
GROUP = 8
TILE = 128
FACTOR = HD**-0.5
LOG2E = 1.4426950408889634
NEGATIVE = -1e30
BF16 = jnp.bfloat16
F32 = jnp.float32


def split3(x):
    high = lax.reduce_precision(x, 8, 7)
    rest = x - high
    middle = lax.reduce_precision(rest, 8, 7)
    return high.astype(BF16), middle.astype(BF16), (rest - middle).astype(BF16)


def attention_kernel(q_ref, k_ref, v_ref, out_ref, lse_ref):
    head = pl.program_id(0)
    groups, rows, _ = q_ref.shape
    total = groups * rows
    keys = k_ref[...]
    values = jnp.concatenate([v_ref[...], jnp.ones((v_ref.shape[0], HD), BF16)], axis=1)
    per = TILE // rows

    def score(at):
        queries = q_ref[at * per : (at + 1) * per].reshape(TILE, HD)
        return lax.dot_general(
            queries, keys, (((1,), (1,)), ((), ())), preferred_element_type=F32
        )

    following = score(0)
    for at in range(total // TILE):
        scores = following
        if (at + 1) * TILE < total:
            following = score(at + 1)
        top = jnp.max(scores, axis=1, keepdims=True)
        weights = jnp.exp2((scores - top) * (FACTOR * LOG2E)).astype(BF16)
        both = jnp.dot(weights, values, preferred_element_type=F32)
        summed = both[:, HD:]
        out_ref[at * per : (at + 1) * per, pl.ds(pl.multiple_of(head * rows, rows), rows), :] = (
            (both[:, :HD] / summed).astype(BF16).reshape(per, rows, HD)
        )
        lse = top * FACTOR + jnp.log(summed)
        for j in range(TILE // 128):
            lse_ref[
                pl.ds(pl.multiple_of(head * 8, 8), 8),
                at * TILE + 128 * j : at * TILE + 128 * j + 128,
            ] = lse[128 * j : 128 * j + 128].T[0:8]

    @pl.when(head == KVH - 1)
    def _():
        row = lax.broadcasted_iota(jnp.int32, (8, total), 0)
        upper = jnp.zeros((8, total), F32)
        lower = upper
        for h in range(KVH):
            whole = lse_ref[8 * h : 8 * h + 8, :]
            high = whole.astype(BF16).astype(F32)
            rest = whole - high
            middle = rest.astype(BF16).astype(F32)
            upper = jnp.where(row == h, high, jnp.where(row == KVH + h, middle, upper))
            lower = jnp.where(row == h, rest - middle, lower)
        parts = jnp.concatenate([upper, lower], axis=0)
        rolled = pltpu.roll(parts, total - rows, 1)
        for r in range(groups):
            source = parts if r % 2 == 0 else rolled
            at = r // 2 * 128
            out_ref[r, KVH * rows :, :] = source[:, at : at + 128].astype(BF16)


def prefix_attention(queries, kv):
    groups, rows, _ = queries.shape
    tokens = kv.shape[0]
    each = rows // KVH
    return pl.pallas_call(
        attention_kernel,
        out_shape=jax.ShapeDtypeStruct((groups, rows + 16, HD), BF16),
        grid=(KVH,),
        in_specs=[
            pl.BlockSpec((groups, each, HD), lambda h: (0, h, 0)),
            pl.BlockSpec((tokens, HD), lambda h: (0, h)),
            pl.BlockSpec((tokens, HD), lambda h: (0, KVH + h)),
        ],
        out_specs=pl.BlockSpec((groups, rows + 16, HD), lambda h: (0, 0, 0)),
        scratch_shapes=[pltpu.VMEM((8 * KVH, groups * each), F32)],
        compiler_params=pltpu.CompilerParams(vmem_limit_bytes=48 * 2**20),
        cost_estimate=pl.CostEstimate(
            flops=4 * groups * rows * tokens * HD,
            bytes_accessed=4 * groups * rows * HD + 4 * tokens * KVH * HD,
            transcendentals=groups * rows * tokens,
        ),
    )(queries, kv, kv)


def suffix_attention(query, suffix_kv, lengths):
    rows = query.shape[0]
    positions = suffix_kv.shape[1]
    shaped = query.reshape(rows, KVH, -1, HD)
    keys = suffix_kv[:, :, : KVH * HD].reshape(rows, positions, KVH, HD)
    values = suffix_kv[:, :, KVH * HD :].reshape(rows, positions, KVH, HD)
    scores = jnp.einsum("rkgd,rskd->rkgs", shaped, keys, preferred_element_type=F32) * FACTOR
    live = jnp.arange(positions, dtype=jnp.int32)[None, :] < lengths[:, None]
    scores = jnp.where(live[:, None, None, :], scores, NEGATIVE)
    top = jnp.max(scores, axis=-1, keepdims=True)
    expo = jnp.exp(scores - top)
    summed = jnp.sum(expo, axis=-1, keepdims=True)
    output = (
        jnp.einsum("rkgs,rskd->rkgd", expo.astype(BF16), values, preferred_element_type=F32)
        / summed
    )
    lse = top + jnp.log(summed)
    return output.reshape(rows, -1, HD), lse.reshape(rows, -1, 1)


def a2a(x, axis, groups=None):
    return lax.all_to_all(x, axis, 0, 0, tiled=True, axis_index_groups=groups)


def local(query, prefix_id, suffix_blocks, prefix_kv, suffix_kv, w_out):
    req = lax.axis_size("req")
    ctx = lax.axis_size("ctx")
    rows = query.shape[0]
    heads = query.shape[1] // HD
    group_rows = rows * ctx
    slots = ctx * SLOTS
    near = [list(range(a, a + GROUP)) for a in range(0, ctx, GROUP)]
    far = [list(range(m, ctx, GROUP)) for m in range(GROUP)]
    width = w_out.shape[1] // GROUP
    share = heads // GROUP
    count = heads * SLOTS
    mine = lax.axis_index("ctx") // GROUP

    with jax.named_scope("split_near"):
        asked = query.reshape(rows, GROUP, share, HD).transpose(1, 2, 0, 3)
        asked = asked.reshape(GROUP, share * rows, HD)
        payload = jnp.concatenate([asked, w_out.T.reshape(GROUP, width, HD)], axis=1)
        payload = a2a(payload, "ctx", near)
        asked = payload[:, : share * rows]
        block = payload[:, share * rows :].transpose(1, 0, 2).reshape(width, GROUP * HD)

    with jax.named_scope("weights"):
        weights = lax.all_gather(block, "req", axis=0, tiled=True)

    with jax.named_scope("gather_far"):
        asked = lax.all_gather(asked, "ctx", axis=0, tiled=True, axis_index_groups=far)
        asked = asked.reshape(ctx, share, rows, HD).transpose(0, 2, 1, 3)
        asked = asked.reshape(group_rows, share * HD)

    with jax.named_scope("slots"):
        index = jnp.arange(group_rows, dtype=jnp.int32)
        same = prefix_id[:, None] == prefix_id[None, :]
        rank = jnp.sum((same & (index[None, :] < index[:, None])).astype(jnp.int32), axis=1)
        slot = prefix_id * SLOTS + rank
        close = jnp.arange(GROUP * SLOTS, dtype=jnp.int32) + mine * (GROUP * SLOTS)
        place = (slot[None, :] == close[:, None]).astype(BF16)
        picked = jnp.dot(place, asked, preferred_element_type=F32).astype(BF16)
        picked = picked.reshape(GROUP, SLOTS, share, HD).transpose(0, 2, 1, 3)
        by_slot = a2a(picked, "ctx", near).reshape(count, HD)

    with jax.named_scope("gather_req"):
        spread = jnp.broadcast_to(by_slot[None], (req, *by_slot.shape))
        gathered = a2a(spread, "req")

    with jax.named_scope("prefix"):
        partials = prefix_attention(gathered, prefix_kv[0])
        received = a2a(partials, "req")

    with jax.named_scope("suffix"):
        own, own_lse = suffix_attention(query, suffix_kv, suffix_blocks[0] * SB)
        own = own.astype(BF16).transpose(1, 0, 2)
        own_lse = own_lse[..., 0].T

    with jax.named_scope("merge"):
        logs = received[:, count : count + 3 * KVH, : count // KVH].astype(F32)
        logs = jnp.sum(logs.reshape(req, 3, count), axis=1)
        peak = jnp.max(logs, axis=0)
        shares = jnp.exp(logs - peak)
        total = jnp.sum(shares, axis=0)
        merged = jnp.sum(shares[..., None] * received[:, :count].astype(F32), axis=0)
        merged = (merged / total[:, None]).astype(BF16)
        merged_lse = (peak + jnp.log(total)).reshape(heads, SLOTS)

    with jax.named_scope("to_heads"):
        each = SLOTS + rows
        parts = jnp.concatenate(split3(jnp.concatenate([merged_lse, own_lse], axis=1)), axis=1)
        parts = jnp.pad(parts, ((0, 0), (0, HD - 3 * each)))[:, None]
        payload = jnp.concatenate(
            [merged.reshape(heads, SLOTS, HD), own, parts, jnp.zeros((heads, 3, HD), BF16)], axis=1
        )
        arrived = a2a(payload, "ctx")

    with jax.named_scope("mix"):
        match = slot[:, None] == jnp.arange(slots, dtype=jnp.int32)[None, :]
        prefix = jnp.dot(
            match.astype(BF16), arrived[:, :SLOTS].reshape(slots, HD), preferred_element_type=F32
        )
        logs = arrived[:, each, : 3 * each].astype(F32).reshape(ctx, 3, each).sum(axis=1)
        prefix_lse = jnp.sum(
            jnp.where(match, logs[:, :SLOTS].reshape(1, slots), 0.0), axis=1, keepdims=True
        )
        own = arrived[:, SLOTS:each].astype(F32).reshape(group_rows, HD)
        own_lse = logs[:, SLOTS:].reshape(group_rows, 1)
        top = jnp.maximum(prefix_lse, own_lse)
        prefix_share = jnp.exp(prefix_lse - top)
        own_share = jnp.exp(own_lse - top)
        attention = (prefix_share * prefix + own_share * own) / (prefix_share + own_share)
        attention = attention.astype(BF16)

    with jax.named_scope("projection"):
        shared = a2a(jnp.broadcast_to(attention[None], (GROUP, *attention.shape)), "ctx", near)
        shared = shared.transpose(1, 0, 2).reshape(group_rows, GROUP * HD)
        terms = lax.dot_general(
            shared, weights, (((1,), (1,)), ((), ())), preferred_element_type=F32
        ).astype(BF16)
        home = a2a(terms.reshape(ctx, rows, -1), "ctx")
        home = home.reshape(ctx // GROUP, GROUP, rows, req, width).astype(F32)
        summed = jnp.sum(home, axis=0).transpose(1, 2, 0, 3)
        return summed.reshape(rows, -1).astype(BF16)


def solution(mesh):
    in_specs = (
        P(("req", "ctx"), None),
        P("req"),
        P(("req", "ctx"), None),
        P("ctx", "req", None),
        P(("req", "ctx"), None, None),
        P("ctx", "req"),
    )
    out_specs = P(("req", "ctx"), None)
    return jax.shard_map(local, mesh=mesh, in_specs=in_specs, out_specs=out_specs, check_vma=False)
```

time: 206 us -> 192 us (0.932)
  blocking collectives: 67.4 us -> 86.4 us
  waiting for transfers between devices: 56.5 us -> 38.2 us
  starting transfers between devices: 39 us -> 25.9 us
  Pallas kernels: 14.2 us -> 8.11 us
  other arithmetic: 1.88 us -> 4.74 us
    all_to_all x5 -> x4, waiting for transfers between devices: 49.9 us -> 27.2 us  [a2a(): return lax.all_to_all(x, axis, 0, 0, tiled=True, axis_index_groups=groups)]
    all_gather x0 -> x1, blocking collectives: none -> 17.8 us  [local(): lax.all_gather(asked, 'ctx', axis=0, tiled=True, axis_index_groups=far)]
    all_to_all x5 -> x4, starting transfers between devices: 38.9 us -> 25.9 us  [a2a(): return lax.all_to_all(x, axis, 0, 0, tiled=True, axis_index_groups=groups)]
    pallas_call x1, Pallas kernels: 14.2 us -> 8.11 us  [prefix_attention(): pl.pallas_call(attention_kernel, out_shape=jax.ShapeDtypeStruct((groups,...]
    all_gather x1, waiting for transfers between devices: 6.58 us -> 11 us  [local(): weights = lax.all_gather(block, 'req', axis=0, tiled=True)]
  transfers between devices with their start and end apart: 6 -> 5, of which waited for: 5 -> 4; matrix products, arithmetic and copies ran while one was open for 2% -> 6% of each run, Pallas kernels for 7% -> 0%
where the time goes in v2:
time: 192 us; the launch traced here: 191 us
  blocking collectives  86.4 us (45%)
  waiting for transfers between devices  38.2 us (20%)
  starting transfers between devices  25.9 us (13%)
  between operations  13.7 us (7%)
  local copies, waits for them, and re-layouts  10.9 us (6%)
  Pallas kernels  8.11 us (4%)
  other arithmetic  4.74 us (2%)
  matrix products  3.04 us (2%)
    all_to_all x3, blocking collectives, a2a(): return lax.all_to_all(x, axis, 0, 0, tiled=True, axis_index_groups=groups)  68.6 us
    all_to_all x4, waiting for transfers between devices, a2a(): return lax.all_to_all(x, axis, 0, 0, tiled=True, axis_index_groups=groups)  27.2 us
    all_to_all x4, starting transfers between devices, a2a(): return lax.all_to_all(x, axis, 0, 0, tiled=True, axis_index_groups=groups)  25.9 us
    all_gather x1, blocking collectives, local(): lax.all_gather(asked, 'ctx', axis=0, tiled=True, axis_index_groups=far)  17.8 us
    all_gather x1, waiting for transfers between devices, local(): weights = lax.all_gather(block, 'req', axis=0, tiled=True)  11 us
    pallas_call x1, Pallas kernels, prefix_attention(): pl.pallas_call(attention_kernel, out_shape=jax.ShapeDtypeStruct((groups,...  8.11 us
  transfers between devices with their start and end apart: 5, of which 4 were waited for; matrix products, arithmetic and copies ran while one was open for 6% of the time, Pallas kernels for 0%

profile of v2, /device:TPU:1, one launch (start us, length us, event | category | flops | bytes accessed | tf_op | source)
XLA Modules:
  0.0 191.0 jit_solution(16189403857036105949)
XLA Ops:
  6.5 1.5 pad_maximum_fusion
  8.1 10.1 %all-to-all-start = ((bf16[8,56,128]{2,1,0:T(8,128)(2,1)}), bf16[8,56,128]{2,1,0:T(8,128)(2,1)S(1)}, u32[]{:S(2)}, u32[]{:S(2)}) async-start(bf16[8,56,128]{2,1,0:T(8,128)(2,1)} %pad_maximum_fusion), calls=%async_computation | async-start | bytes 229376 | tf_op jit(solution)/shard_map/split_near/all_to_all | solution.py:128
  18.2 0.9 convert_reduce_fusion
  19.1 0.7 multiply_add_fusion
  19.8 4.2 %all-to-all-done = bf16[8,56,128]{2,1,0:T(8,128)(2,1)S(1)} async-done(((bf16[8,56,128]{2,1,0:T(8,128)(2,1)}), bf16[8,56,128]{2,1,0:T(8,128)(2,1)S(1)}, u32[]{:S(2)}, u32[]{:S(2)}) %all-to-all-start) | async-done | bytes 114720 | tf_op jit(solution)/shard_map/split_near/all_to_all | solution.py:128
  23.9 17.8 %all_gather.6 = bf16[32,16,128]{2,1,0:T(8,128)(2,1)S(1)} all-gather(bf16[8,16,128]{2,1,0:T(8,128)(2,1)S(1)} %slice.44), channel_id=1, replica_groups={{0,8,16,24},{1,9,17,25},{2,10,18,26},{3,11,19,27},{4,12,20,28},{5,13,21..., dimensions={0}, use_global_device_ids=true | all-gather | bytes 163840 | tf_op jit(solution)/shard_map/gather_far/all_gather | solution.py:157
  42.0 11.5 %all_to_all.35 = bf16[8,4,8,128]{3,2,1,0:T(8,128)(2,1)S(1)} all-to-all(bf16[8,4,8,128]{3,2,1,0:T(8,128)(2,1)S(1)} %fusion.1), channel_id=1, replica_groups={{0,1,2,3,4,5,6,7},{8,9,10,11,12,13,14,15},{16,17,18,19,20,21,22,23},{24..., dimensions={0} | all-to-all | bytes 131072 | tf_op jit(solution)/shard_map/slots/all_to_all | solution.py:128
  53.5 1.2 broadcast_in_dim.37
  54.8 6.9 %all-to-all-start.2 = ((bf16[16,256,128]{2,1,0:T(8,128)(2,1)}), bf16[16,256,128]{2,1,0:T(8,128)(2,1)S(1)}, u32[]{:S(2)}, u32[]{:S(2)}) async-start(bf16[16,256,128]{2,1,0:T(8,128)(2,1)} %broadcast_in_dim.37), calls=%async_computation.2 | async-start | bytes 2097152 | tf_op jit(solution)/shard_map/gather_req/all_to_all | solution.py:128
  61.7 3.1 %fusion.34 = (bf16[4,256,512]{2,1,0:T(8,128)(2,1)}, bf16[4,256,512]{2,1,0:T(8,128)(2,1)}) fusion(bf16[4,256,1024]{2,1,0:T(8,128)(2,1)} %param.10), kind=kLoop, calls=%fused_computation.67 | loop fusion | bytes 4194304 | tf_op jit(solution)/shard_map/suffix/slice | solution.py:112
  64.8 12.2 %all-to-all-done.2.q_ref = bf16[16,256,128]{2,1,0:T(8,128)(2,1)S(1)} async-done(((bf16[16,256,128]{2,1,0:T(8,128)(2,1)}), bf16[16,256,128]{2,1,0:T(8,128)(2,1)S(1)}, u32[]{:S(2)}, u32[]{:S(2)}) %all-to-all-start.2) | async-done | bytes 1048608 | tf_op jit(solution)/shard_map/gather_req/all_to_all | solution.py:128
  77.0 8.1 %prefix.1 = bf16[16,272,128]{2,1,0:T(8,128)(2,1)} custom-call(bf16[16,256,128]{2,1,0:T(8,128)(2,1)S(1)} %all-to-all-done.2.q_ref, bf16[1024,1024]{1,0:T(8,128)(2,1)S(1)} %bitcast.70, bf16[1024,1024]{1,0:T(8,128)(2,1)S(1)} %bitcast.71), custom_call_target="tpu_custom_call" | custom-call | flops 2147483648 | bytes 4194304 | tf_op jit(solution)/shard_map/prefix/pallas_call | solution.py:87
  85.1 3.9 %all-to-all-start.3 = ((bf16[16,272,128]{2,1,0:T(8,128)(2,1)}), bf16[16,272,128]{2,1,0:T(8,128)(2,1)S(1)}, u32[]{:S(2)}, u32[]{:S(2)}) async-start(bf16[16,272,128]{2,1,0:T(8,128)(2,1)} %prefix.1), calls=%async_computation.3 | async-start | bytes 2228224 | tf_op jit(solution)/shard_map/prefix/all_to_all | solution.py:128
  89.2 1.6 copy.153
  93.1 10.9 %all-to-all-done.3 = bf16[16,272,128]{2,1,0:T(8,128)(2,1)S(1)} async-done(((bf16[16,272,128]{2,1,0:T(8,128)(2,1)}), bf16[16,272,128]{2,1,0:T(8,128)(2,1)S(1)}, u32[]{:S(2)}, u32[]{:S(2)}) %all-to-all-start.3) | async-done | bytes 1114144 | tf_op jit(solution)/shard_map/prefix/all_to_all | solution.py:128
  104.5 0.7 multiply_reduce_fusion
  105.6 26.3 %all_to_all.36 = bf16[32,16,128]{2,1,0:T(8,128)(2,1)S(1)} all-to-all(bf16[32,16,128]{2,1,0:T(8,128)(2,1)S(1)} %maximum_maximum_fusion), channel_id=1, replica_groups=mesh['req'=16,'ctx'=32] {'ctx'}, dimensions={0} | all-to-all | bytes 262144 | tf_op jit(solution)/shard_map/to_heads/all_to_all | solution.py:128
  133.0 0.8 broadcast_in_dim.71
  133.7 4.9 %all-to-all-start.5 = ((bf16[8,128,128]{1,2,0:T(8,128)(2,1)}), bf16[8,128,128]{1,2,0:T(8,128)(2,1)S(1)}, u32[]{:S(2)}, u32[]{:S(2)}) async-start(bf16[8,128,128]{1,2,0:T(8,128)(2,1)} %broadcast_in_dim.71), calls=%async_computation.5 | async-start | bytes 524288 | tf_op jit(solution)/shard_map/projection/all_to_all | solution.py:128
  138.6 11.0 %all-gather.2.cloned.1.call-done = bf16[640,1024]{1,0:T(8,128)(2,1)} async-done(((bf16[40,1024]{1,0:T(8,128)(2,1)}), bf16[640,1024]{1,0:T(8,128)(2,1)}) %all-gather.2.cloned.1.call-update) | async-done | bytes 1310736 | tf_op jit(solution)/shard_map/weights/all_gather | solution.py:154
  149.6 1.9 convolution_convert_fusion
  151.5 30.8 %all_to_all.37 = bf16[32,4,640]{2,1,0:T(4,128)(2,1)S(1)} all-to-all(bf16[32,4,640]{2,1,0:T(4,128)(2,1)S(1)} %reshape.193), channel_id=1, replica_groups=mesh['req'=16,'ctx'=32] {'ctx'}, dimensions={0} | all-to-all | bytes 327680 | tf_op jit(solution)/shard_map/projection/all_to_all | solution.py:128
  182.3 0.8 convert_element_type.83
  183.3 0.8 convert_element_type.87
  (61 shorter events, 4.8 us)
Async XLA Ops:
  8.1 15.9 %all-to-all-start = ((bf16[8,56,128]{2,1,0:T(8,128)(2,1)}), bf16[8,56,128]{2,1,0:T(8,128)(2,1)S(1)}, u32[]{:S(2)}, u32[]{:S(2)}) async-start(bf16[8,56,128]{2,1,0:T(8,128)(2,1)} %pad_maximum_fusion), calls=%async_computation | async-start | bytes 229376 | tf_op jit(solution)/shard_map/split_near/all_to_all | solution.py:128
  54.8 6.9 %copy-start.3 = (s32[1,4]{1,0:T(1,128)S(1)}, s32[1,4]{1,0:T(1,128)}, u32[]{:S(2)}) copy-start(s32[1,4]{1,0:T(1,128)} %param.8) | copy-start | bytes 52
  54.8 22.2 %all-to-all-start.2 = ((bf16[16,256,128]{2,1,0:T(8,128)(2,1)}), bf16[16,256,128]{2,1,0:T(8,128)(2,1)S(1)}, u32[]{:S(2)}, u32[]{:S(2)}) async-start(bf16[16,256,128]{2,1,0:T(8,128)(2,1)} %broadcast_in_dim.37), calls=%async_computation.2 | async-start | bytes 2097152 | tf_op jit(solution)/shard_map/gather_req/all_to_all | solution.py:128
  61.7 15.3 %copy-start = (bf16[1,1024,1024]{2,1,0:T(8,128)(2,1)S(1)}, bf16[1,1024,1024]{2,1,0:T(8,128)(2,1)}, u32[]{:S(2)}) copy-start(bf16[1,1024,1024]{2,1,0:T(8,128)(2,1)} %param.9) | copy-start | bytes 6291460
  85.1 18.9 %all-to-all-start.3 = ((bf16[16,272,128]{2,1,0:T(8,128)(2,1)}), bf16[16,272,128]{2,1,0:T(8,128)(2,1)S(1)}, u32[]{:S(2)}, u32[]{:S(2)}) async-start(bf16[16,272,128]{2,1,0:T(8,128)(2,1)} %prefix.1), calls=%async_computation.3 | async-start | bytes 2228224 | tf_op jit(solution)/shard_map/prefix/all_to_all | solution.py:128
  89.1 1.7 copy-start.2
  89.1 60.5 %all-gather.2.cloned.1.call-start = ((), (), s32[]{:S(2)}) async-start(), calls=%async_computation.7 | async-start | bytes 1392640 | tf_op jit(solution)/shard_map/weights/all_gather | solution.py:154
  89.2 2.2 %copy-start.1 = (bf16[4,256,512]{2,1,0:T(8,128)(2,1)S(1)}, bf16[4,256,512]{2,1,0:T(8,128)(2,1)}, u32[]{:S(2)}) copy-start(bf16[4,256,512]{2,1,0:T(8,128)(2,1)} %get-tuple-element.10) | copy-start | bytes 3145732
  133.7 15.9 %all-to-all-start.5 = ((bf16[8,128,128]{1,2,0:T(8,128)(2,1)}), bf16[8,128,128]{1,2,0:T(8,128)(2,1)S(1)}, u32[]{:S(2)}, u32[]{:S(2)}) async-start(bf16[8,128,128]{1,2,0:T(8,128)(2,1)} %broadcast_in_dim.71), calls=%async_computation.5 | async-start | bytes 524288 | tf_op jit(solution)/shard_map/projection/all_to_all | solution.py:128
Sparse Core Ops, SparseCore 0:
  93.3 56.2 all-gather.1

commit v3 on v2

--- a/solution.py
+++ b/solution.py
@@ -175,6 +175,7 @@
 
     with jax.named_scope("prefix"):
         partials = prefix_attention(gathered, prefix_kv[0])
+        partials, weights = lax.optimization_barrier((partials, weights))
         received = a2a(partials, "req")
 
     with jax.named_scope("suffix"):

time: 192 us -> 182 us (0.948)
  blocking collectives: 86.4 us -> 109 us
  waiting for transfers between devices: 38.2 us -> 21.8 us
  starting transfers between devices: 25.9 us -> 12.6 us
    all_to_all x3 -> x5, blocking collectives: 68.6 us -> 90.8 us  [a2a(): return lax.all_to_all(x, axis, 0, 0, tiled=True, axis_index_groups=groups)]
    all_to_all x4 -> x2, starting transfers between devices: 25.9 us -> 12.6 us  [a2a(): return lax.all_to_all(x, axis, 0, 0, tiled=True, axis_index_groups=groups)]
    all_gather x1, waiting for transfers between devices: 11 us -> 0.01 us  [local(): weights = lax.all_gather(block, 'req', axis=0, tiled=True)]
    all_to_all x4 -> x2, waiting for transfers between devices: 27.2 us -> 21.8 us  [a2a(): return lax.all_to_all(x, axis, 0, 0, tiled=True, axis_index_groups=groups)]
  transfers between devices with their start and end apart: 5 -> 3, of which waited for: 4 -> 2; matrix products, arithmetic and copies ran while one was open for 6% -> 5% of each run, Pallas kernels for 0% -> 4%
where the time goes in v3:
time: 182 us; the launch traced here: 181 us
  blocking collectives  109 us (60%)
  waiting for transfers between devices  21.8 us (12%)
  between operations  13.7 us (8%)
  starting transfers between devices  12.6 us (7%)
  local copies, waits for them, and re-layouts  10.2 us (6%)
  Pallas kernels  8.12 us (4%)
  other arithmetic  4.11 us (2%)
    all_to_all x5, blocking collectives, a2a(): return lax.all_to_all(x, axis, 0, 0, tiled=True, axis_index_groups=groups)  90.8 us
    all_to_all x2, waiting for transfers between devices, a2a(): return lax.all_to_all(x, axis, 0, 0, tiled=True, axis_index_groups=groups)  21.8 us
    all_gather x1, blocking collectives, local(): lax.all_gather(asked, 'ctx', axis=0, tiled=True, axis_index_groups=far)  18.4 us
    all_to_all x2, starting transfers between devices, a2a(): return lax.all_to_all(x, axis, 0, 0, tiled=True, axis_index_groups=groups)  12.6 us
    pallas_call x1, Pallas kernels, prefix_attention(): pl.pallas_call(attention_kernel, out_shape=jax.ShapeDtypeStruct((groups,...  8.12 us
  transfers between devices with their start and end apart: 3, of which 2 were waited for; matrix products, arithmetic and copies ran while one was open for 5% of the time, Pallas kernels for 4%

profile of v3, /device:TPU:1, one launch (start us, length us, event | category | flops | bytes accessed | tf_op | source)
XLA Modules:
  0.0 181.4 jit_solution(1195433945447232650)
XLA Ops:
  6.5 0.9 pad_maximum_fusion
  7.4 15.0 %all_to_all.35 = bf16[8,56,128]{2,1,0:T(8,128)(2,1)S(1)} all-to-all(bf16[8,56,128]{2,1,0:T(8,128)(2,1)S(1)} %pad_maximum_fusion), channel_id=1, replica_groups={{0,1,2,3,4,5,6,7},{8,9,10,11,12,13,14,15},{16,17,18,19,20,21,22,23},{24..., dimensions={0} | all-to-all | bytes 229376 | tf_op jit(solution)/shard_map/split_near/all_to_all | solution.py:128
  22.4 0.6 copy_bitcast_fusion
  23.1 0.9 convert_reduce_fusion
  24.0 0.7 multiply_add_fusion
  24.7 18.4 %all_gather.6 = bf16[32,16,128]{2,1,0:T(8,128)(2,1)S(1)} all-gather(bf16[8,16,128]{2,1,0:T(8,128)(2,1)S(1)} %slice.44), channel_id=1, replica_groups={{0,8,16,24},{1,9,17,25},{2,10,18,26},{3,11,19,27},{4,12,20,28},{5,13,21..., dimensions={0}, use_global_device_ids=true | all-gather | bytes 163840 | tf_op jit(solution)/shard_map/gather_far/all_gather | solution.py:157
  43.4 11.5 %all_to_all.36 = bf16[8,4,8,128]{3,2,1,0:T(8,128)(2,1)S(1)} all-to-all(bf16[8,4,8,128]{3,2,1,0:T(8,128)(2,1)S(1)} %fusion.1), channel_id=1, replica_groups={{0,1,2,3,4,5,6,7},{8,9,10,11,12,13,14,15},{16,17,18,19,20,21,22,23},{24..., dimensions={0} | all-to-all | bytes 131072 | tf_op jit(solution)/shard_map/slots/all_to_all | solution.py:128
  54.8 1.2 broadcast_in_dim.37
  56.0 6.8 %all-to-all-start.2 = ((bf16[16,256,128]{2,1,0:T(8,128)(2,1)}), bf16[16,256,128]{2,1,0:T(8,128)(2,1)S(1)}, u32[]{:S(2)}, u32[]{:S(2)}) async-start(bf16[16,256,128]{2,1,0:T(8,128)(2,1)} %broadcast_in_dim.37), calls=%async_computation.2 | async-start | bytes 2097152 | tf_op jit(solution)/shard_map/gather_req/all_to_all | solution.py:128
  62.8 3.1 %fusion.34 = (bf16[4,256,512]{2,1,0:T(8,128)(2,1)}, bf16[4,256,512]{2,1,0:T(8,128)(2,1)}) fusion(bf16[4,256,1024]{2,1,0:T(8,128)(2,1)} %param.10), kind=kLoop, calls=%fused_computation.67 | loop fusion | bytes 4194304 | tf_op jit(solution)/shard_map/suffix/slice | solution.py:112
  66.0 13.0 %all-to-all-done.2.q_ref = bf16[16,256,128]{2,1,0:T(8,128)(2,1)S(1)} async-done(((bf16[16,256,128]{2,1,0:T(8,128)(2,1)}), bf16[16,256,128]{2,1,0:T(8,128)(2,1)S(1)}, u32[]{:S(2)}, u32[]{:S(2)}) %all-to-all-start.2) | async-done | bytes 1048608 | tf_op jit(solution)/shard_map/gather_req/all_to_all | solution.py:128
  78.9 8.1 %prefix.1 = bf16[16,272,128]{2,1,0:T(8,128)(2,1)} custom-call(bf16[16,256,128]{2,1,0:T(8,128)(2,1)S(1)} %all-to-all-done.2.q_ref, bf16[1024,1024]{1,0:T(8,128)(2,1)S(1)} %bitcast.70, bf16[1024,1024]{1,0:T(8,128)(2,1)S(1)} %bitcast.71), custom_call_target="tpu_custom_call" | custom-call | flops 2147483648 | bytes 4194304 | tf_op jit(solution)/shard_map/prefix/pallas_call | solution.py:87
  87.0 5.8 %all-to-all-start.3 = ((bf16[16,272,128]{2,1,0:T(8,128)(2,1)}), bf16[16,272,128]{2,1,0:T(8,128)(2,1)S(1)}, u32[]{:S(2)}, u32[]{:S(2)}) async-start(bf16[16,272,128]{2,1,0:T(8,128)(2,1)} %prefix.1), calls=%async_computation.3 | async-start | bytes 2228224 | tf_op jit(solution)/shard_map/prefix/all_to_all | solution.py:128
  92.9 1.6 copy.153
  95.2 0.5 copy.154
  95.7 0.4 fusion.6
  96.3 8.8 %all-to-all-done.3 = bf16[16,272,128]{2,1,0:T(8,128)(2,1)S(1)} async-done(((bf16[16,272,128]{2,1,0:T(8,128)(2,1)}), bf16[16,272,128]{2,1,0:T(8,128)(2,1)S(1)}, u32[]{:S(2)}, u32[]{:S(2)}) %all-to-all-start.3) | async-done | bytes 1114144 | tf_op jit(solution)/shard_map/prefix/all_to_all | solution.py:128
  105.5 0.7 multiply_reduce_fusion
  106.6 29.8 %all_to_all.37 = bf16[32,16,128]{2,1,0:T(8,128)(2,1)S(1)} all-to-all(bf16[32,16,128]{2,1,0:T(8,128)(2,1)S(1)} %maximum_maximum_fusion), channel_id=1, replica_groups=mesh['req'=16,'ctx'=32] {'ctx'}, dimensions={0} | all-to-all | bytes 262144 | tf_op jit(solution)/shard_map/to_heads/all_to_all | solution.py:128
  137.6 12.7 %all_to_all.38 = bf16[8,128,128]{1,2,0:T(8,128)(2,1)S(1)} all-to-all(bf16[8,128,128]{1,2,0:T(8,128)(2,1)S(1)} %broadcast_in_dim.71), channel_id=1, replica_groups={{0,1,2,3,4,5,6,7},{8,9,10,11,12,13,14,15},{16,17,18,19,20,21,22,23},{24..., dimensions={0} | all-to-all | bytes 524288 | tf_op jit(solution)/shard_map/projection/all_to_all | solution.py:128
  150.3 0.5 convolution_convert_fusion
  150.9 21.8 %all_to_all.39 = bf16[32,4,640]{2,1,0:T(4,128)(2,1)S(1)} all-to-all(bf16[32,4,640]{2,1,0:T(4,128)(2,1)S(1)} %reshape.193), channel_id=1, replica_groups=mesh['req'=16,'ctx'=32] {'ctx'}, dimensions={0} | all-to-all | bytes 327680 | tf_op jit(solution)/shard_map/projection/all_to_all | solution.py:128
  172.7 0.8 convert_element_type.83
  173.7 0.8 convert_element_type.87
  (61 shorter events, 3.2 us)
Async XLA Ops:
  6.5 80.5 %all-gather.2.cloned.1.call-start = ((), (), s32[]{:S(2)}) async-start(), calls=%async_computation.7 | async-start | bytes 1392640 | tf_op jit(solution)/shard_map/weights/all_gather | solution.py:154
  56.0 22.9 %all-to-all-start.2 = ((bf16[16,256,128]{2,1,0:T(8,128)(2,1)}), bf16[16,256,128]{2,1,0:T(8,128)(2,1)S(1)}, u32[]{:S(2)}, u32[]{:S(2)}) async-start(bf16[16,256,128]{2,1,0:T(8,128)(2,1)} %broadcast_in_dim.37), calls=%async_computation.2 | async-start | bytes 2097152 | tf_op jit(solution)/shard_map/gather_req/all_to_all | solution.py:128
  62.8 16.1 %copy-start = (bf16[1,1024,1024]{2,1,0:T(8,128)(2,1)S(1)}, bf16[1,1024,1024]{2,1,0:T(8,128)(2,1)}, u32[]{:S(2)}) copy-start(bf16[1,1024,1024]{2,1,0:T(8,128)(2,1)} %param.9) | copy-start | bytes 6291460
  87.0 5.8 %copy-start.4 = (s32[1,4]{1,0:T(1,128)S(1)}, s32[1,4]{1,0:T(1,128)}, u32[]{:S(2)}) copy-start(s32[1,4]{1,0:T(1,128)} %param.8) | copy-start | bytes 52
  87.0 18.0 %all-to-all-start.3 = ((bf16[16,272,128]{2,1,0:T(8,128)(2,1)}), bf16[16,272,128]{2,1,0:T(8,128)(2,1)S(1)}, u32[]{:S(2)}, u32[]{:S(2)}) async-start(bf16[16,272,128]{2,1,0:T(8,128)(2,1)} %prefix.1), calls=%async_computation.3 | async-start | bytes 2228224 | tf_op jit(solution)/shard_map/prefix/all_to_all | solution.py:128
  92.9 1.7 copy-start.3
  92.9 2.3 %copy-start.1 = (bf16[4,256,512]{2,1,0:T(8,128)(2,1)S(1)}, bf16[4,256,512]{2,1,0:T(8,128)(2,1)}, u32[]{:S(2)}) copy-start(bf16[4,256,512]{2,1,0:T(8,128)(2,1)} %get-tuple-element.14) | copy-start | bytes 3145732
  106.2 44.1 %copy-start.2 = (bf16[640,1024]{1,0:T(8,128)(2,1)S(1)}, bf16[640,1024]{1,0:T(8,128)(2,1)}, u32[]{:S(2)}) copy-start(bf16[640,1024]{1,0:T(8,128)(2,1)} %all-gather.2.cloned.1.call-done) | copy-start | bytes 3932164
Sparse Core Ops, SparseCore 0:
  23.2 62.5 all-gather.1

commit v4 on v2

--- a/solution.py
+++ b/solution.py
@@ -151,7 +151,8 @@
         block = payload[:, share * rows :].transpose(1, 0, 2).reshape(width, GROUP * HD)
 
     with jax.named_scope("weights"):
-        weights = lax.all_gather(block, "req", axis=0, tiled=True)
+        weights = a2a(jnp.broadcast_to(block[None], (req, *block.shape)), "req")
+        weights = weights.reshape(req * width, GROUP * HD)
 
     with jax.named_scope("gather_far"):
         asked = lax.all_gather(asked, "ctx", axis=0, tiled=True, axis_index_groups=far)
@@ -167,6 +168,7 @@
         place = (slot[None, :] == close[:, None]).astype(BF16)
         picked = jnp.dot(place, asked, preferred_element_type=F32).astype(BF16)
         picked = picked.reshape(GROUP, SLOTS, share, HD).transpose(0, 2, 1, 3)
+        picked, weights = lax.optimization_barrier((picked, weights))
         by_slot = a2a(picked, "ctx", near).reshape(count, HD)
 
     with jax.named_scope("gather_req"):

time: 192 us -> 173 us (0.901)
  blocking collectives: 86.4 us -> 108 us
  waiting for transfers between devices: 38.2 us -> 23.7 us
  between operations: 13.7 us -> 0.36 us
  starting transfers between devices: 25.9 us -> 16.7 us
  other arithmetic: 4.74 us -> 2.72 us
    all_to_all x3 -> x5, blocking collectives: 68.6 us -> 86.8 us  [a2a(): return lax.all_to_all(x, axis, 0, 0, tiled=True, axis_index_groups=groups)]
    all_gather x1 -> x0, waiting for transfers between devices: 11 us -> none  [local(): weights = lax.all_gather(block, 'req', axis=0, tiled=True)]
    all_to_all x4 -> x3, starting transfers between devices: 25.9 us -> 16.7 us  [a2a(): return lax.all_to_all(x, axis, 0, 0, tiled=True, axis_index_groups=groups)]
    all_to_all x4 -> x3, waiting for transfers between devices: 27.2 us -> 23.7 us  [a2a(): return lax.all_to_all(x, axis, 0, 0, tiled=True, axis_index_groups=groups)]
    all_gather x1, blocking collectives: 17.8 us -> 21 us  [local(): lax.all_gather(asked, 'ctx', axis=0, tiled=True, axis_index_groups=far)]
  transfers between devices with their start and end apart: 5 -> 3, of which waited for: 4 -> 2; matrix products, arithmetic and copies ran while one was open for 6% -> 4% of each run, Pallas kernels for 0% -> 0%
where the time goes in v4:
time: 173 us; the launch traced here: 172 us
  blocking collectives  108 us (62%)
  waiting for transfers between devices  23.7 us (14%)
  starting transfers between devices  16.7 us (10%)
  local copies, waits for them, and re-layouts  10.8 us (6%)
  Pallas kernels  8.12 us (5%)
  other arithmetic  2.72 us (2%)
    all_to_all x5, blocking collectives, a2a(): return lax.all_to_all(x, axis, 0, 0, tiled=True, axis_index_groups=groups)  86.8 us
    all_to_all x3, waiting for transfers between devices, a2a(): return lax.all_to_all(x, axis, 0, 0, tiled=True, axis_index_groups=groups)  23.7 us
    all_gather x1, blocking collectives, local(): lax.all_gather(asked, 'ctx', axis=0, tiled=True, axis_index_groups=far)  21 us
    all_to_all x3, starting transfers between devices, a2a(): return lax.all_to_all(x, axis, 0, 0, tiled=True, axis_index_groups=groups)  16.7 us
    pallas_call x1, Pallas kernels, prefix_attention(): pl.pallas_call(attention_kernel, out_shape=jax.ShapeDtypeStruct((groups,...  8.12 us
  transfers between devices with their start and end apart: 3, of which 2 were waited for; matrix products, arithmetic and copies ran while one was open for 4% of the time, Pallas kernels for 0%

profile of v4, /device:TPU:1, one launch (start us, length us, event | category | flops | bytes accessed | tf_op | source)
XLA Modules:
  0.0 172.0 jit_solution(217281190279988577)
XLA Ops:
  0.0 0.9 pad_maximum_fusion
  0.9 15.0 %all_to_all.40 = bf16[8,56,128]{2,1,0:T(8,128)(2,1)S(1)} all-to-all(bf16[8,56,128]{2,1,0:T(8,128)(2,1)S(1)} %pad_maximum_fusion), channel_id=1, replica_groups={{0,1,2,3,4,5,6,7},{8,9,10,11,12,13,14,15},{16,17,18,19,20,21,22,23},{24..., dimensions={0} | all-to-all | bytes 229376 | tf_op jit(solution)/shard_map/split_near/all_to_all | solution.py:128
  15.9 1.2 broadcast_in_dim.41
  17.1 4.8 %all-to-all-start.1 = ((bf16[16,40,1024]{2,1,0:T(8,128)(2,1)}), bf16[16,40,1024]{2,1,0:T(8,128)(2,1)S(1)}, u32[]{:S(2)}, u32[]{:S(2)}) async-start(bf16[16,40,1024]{2,1,0:T(8,128)(2,1)} %broadcast_in_dim.41), calls=%async_computation.1 | async-start | bytes 2621440 | tf_op jit(solution)/shard_map/weights/all_to_all | solution.py:128
  22.2 21.0 %all_gather.3 = bf16[32,16,128]{2,1,0:T(8,128)(2,1)S(1)} all-gather(bf16[8,16,128]{2,1,0:T(8,128)(2,1)S(1)} %slice.44), channel_id=1, replica_groups={{0,8,16,24},{1,9,17,25},{2,10,18,26},{3,11,19,27},{4,12,20,28},{5,13,21..., dimensions={0}, use_global_device_ids=true | all-gather | bytes 163840 | tf_op jit(solution)/shard_map/gather_far/all_gather | solution.py:158
  43.4 11.0 %all_to_all.41 = bf16[8,4,8,128]{3,2,1,0:T(8,128)(2,1)S(1)} all-to-all(bf16[8,4,8,128]{3,2,1,0:T(8,128)(2,1)S(1)} %fusion.1), channel_id=1, replica_groups={{0,1,2,3,4,5,6,7},{8,9,10,11,12,13,14,15},{16,17,18,19,20,21,22,23},{24..., dimensions={0} | all-to-all | bytes 131072 | tf_op jit(solution)/shard_map/slots/all_to_all | solution.py:128
  54.5 1.2 broadcast_in_dim.43
  55.7 7.8 %all-to-all-start.3 = ((bf16[16,256,128]{2,1,0:T(8,128)(2,1)}), bf16[16,256,128]{2,1,0:T(8,128)(2,1)S(1)}, u32[]{:S(2)}, u32[]{:S(2)}) async-start(bf16[16,256,128]{2,1,0:T(8,128)(2,1)} %broadcast_in_dim.43), calls=%async_computation.3 | async-start | bytes 2097152 | tf_op jit(solution)/shard_map/gather_req/all_to_all | solution.py:128
  63.5 3.1 %fusion.34 = (bf16[4,256,512]{2,1,0:T(8,128)(2,1)}, bf16[4,256,512]{2,1,0:T(8,128)(2,1)}) fusion(bf16[4,256,1024]{2,1,0:T(8,128)(2,1)} %param.10), kind=kLoop, calls=%fused_computation.67 | loop fusion | bytes 4194304 | tf_op jit(solution)/shard_map/suffix/slice | solution.py:112
  66.7 12.2 %all-to-all-done.3.q_ref = bf16[16,256,128]{2,1,0:T(8,128)(2,1)S(1)} async-done(((bf16[16,256,128]{2,1,0:T(8,128)(2,1)}), bf16[16,256,128]{2,1,0:T(8,128)(2,1)S(1)}, u32[]{:S(2)}, u32[]{:S(2)}) %all-to-all-start.3) | async-done | bytes 1048608 | tf_op jit(solution)/shard_map/gather_req/all_to_all | solution.py:128
  78.8 8.1 %prefix.1 = bf16[16,272,128]{2,1,0:T(8,128)(2,1)} custom-call(bf16[16,256,128]{2,1,0:T(8,128)(2,1)S(1)} %all-to-all-done.3.q_ref, bf16[1024,1024]{1,0:T(8,128)(2,1)S(1)} %bitcast.71, bf16[1024,1024]{1,0:T(8,128)(2,1)S(1)} %bitcast.72), custom_call_target="tpu_custom_call" | custom-call | flops 2147483648 | bytes 4194304 | tf_op jit(solution)/shard_map/prefix/pallas_call | solution.py:87
  87.0 4.1 %all-to-all-start.4 = ((bf16[16,272,128]{2,1,0:T(8,128)(2,1)}), bf16[16,272,128]{2,1,0:T(8,128)(2,1)S(1)}, u32[]{:S(2)}, u32[]{:S(2)}) async-start(bf16[16,272,128]{2,1,0:T(8,128)(2,1)} %prefix.1), calls=%async_computation.4 | async-start | bytes 2228224 | tf_op jit(solution)/shard_map/prefix/all_to_all | solution.py:128
  91.1 1.6 copy.153
  92.7 0.3 fusion.35
  93.3 0.5 copy.154
  93.9 0.4 fusion.6
  94.4 11.6 %all-to-all-done.4 = bf16[16,272,128]{2,1,0:T(8,128)(2,1)S(1)} async-done(((bf16[16,272,128]{2,1,0:T(8,128)(2,1)}), bf16[16,272,128]{2,1,0:T(8,128)(2,1)S(1)}, u32[]{:S(2)}, u32[]{:S(2)}) %all-to-all-start.4) | async-done | bytes 1114144 | tf_op jit(solution)/shard_map/prefix/all_to_all | solution.py:128
  106.4 0.7 multiply_reduce_fusion
  107.6 26.3 %all_to_all.42 = bf16[32,16,128]{2,1,0:T(8,128)(2,1)S(1)} all-to-all(bf16[32,16,128]{2,1,0:T(8,128)(2,1)S(1)} %maximum_maximum_fusion), channel_id=1, replica_groups=mesh['req'=16,'ctx'=32] {'ctx'}, dimensions={0} | all-to-all | bytes 262144 | tf_op jit(solution)/shard_map/to_heads/all_to_all | solution.py:128
  135.0 12.7 %all_to_all.43 = bf16[8,128,128]{1,2,0:T(8,128)(2,1)S(1)} all-to-all(bf16[8,128,128]{1,2,0:T(8,128)(2,1)S(1)} %broadcast_in_dim.80), channel_id=1, replica_groups={{0,1,2,3,4,5,6,7},{8,9,10,11,12,13,14,15},{16,17,18,19,20,21,22,23},{24..., dimensions={0} | all-to-all | bytes 524288 | tf_op jit(solution)/shard_map/projection/all_to_all | solution.py:128
  147.7 0.5 convolution_convert_fusion
  148.3 21.8 %all_to_all.44 = bf16[32,4,640]{2,1,0:T(4,128)(2,1)S(1)} all-to-all(bf16[32,4,640]{2,1,0:T(4,128)(2,1)S(1)} %reshape.195), channel_id=1, replica_groups=mesh['req'=16,'ctx'=32] {'ctx'}, dimensions={0} | all-to-all | bytes 327680 | tf_op jit(solution)/shard_map/projection/all_to_all | solution.py:128
  170.1 0.8 convert_element_type.83
  171.1 0.8 convert_element_type.87
  (65 shorter events, 3.1 us)
Async XLA Ops:
  17.1 4.9 %copy-start.5 = (s32[128]{0:T(128)S(1)}, s32[128]{0:T(128)}, u32[]{:S(2)}) copy-start(s32[128]{0:T(128)} %param.7) | copy-start | bytes 1540
  17.1 26.3 %all-to-all-start.1 = ((bf16[16,40,1024]{2,1,0:T(8,128)(2,1)}), bf16[16,40,1024]{2,1,0:T(8,128)(2,1)S(1)}, u32[]{:S(2)}, u32[]{:S(2)}) async-start(bf16[16,40,1024]{2,1,0:T(8,128)(2,1)} %broadcast_in_dim.41), calls=%async_computation.1 | async-start | bytes 2621440 | tf_op jit(solution)/shard_map/weights/all_to_all | solution.py:128
  43.4 12.2 %copy-start.1 = (bf16[16,40,1024]{2,1,0:T(8,128)(2,1)}, bf16[16,40,1024]{2,1,0:T(8,128)(2,1)S(1)}, u32[]{:S(2)}) copy-start(bf16[16,40,1024]{2,1,0:T(8,128)(2,1)S(1)} %all-to-all-done.1) | copy-start | bytes 3932164
  55.7 23.2 %all-to-all-start.3 = ((bf16[16,256,128]{2,1,0:T(8,128)(2,1)}), bf16[16,256,128]{2,1,0:T(8,128)(2,1)S(1)}, u32[]{:S(2)}, u32[]{:S(2)}) async-start(bf16[16,256,128]{2,1,0:T(8,128)(2,1)} %broadcast_in_dim.43), calls=%async_computation.3 | async-start | bytes 2097152 | tf_op jit(solution)/shard_map/gather_req/all_to_all | solution.py:128
  63.5 15.3 %copy-start = (bf16[1,1024,1024]{2,1,0:T(8,128)(2,1)S(1)}, bf16[1,1024,1024]{2,1,0:T(8,128)(2,1)}, u32[]{:S(2)}) copy-start(bf16[1,1024,1024]{2,1,0:T(8,128)(2,1)} %param.9) | copy-start | bytes 6291460
  87.0 4.1 %copy-start.6 = (s32[1,4]{1,0:T(1,128)S(1)}, s32[1,4]{1,0:T(1,128)}, u32[]{:S(2)}) copy-start(s32[1,4]{1,0:T(1,128)} %param.8) | copy-start | bytes 52
  87.0 19.0 %all-to-all-start.4 = ((bf16[16,272,128]{2,1,0:T(8,128)(2,1)}), bf16[16,272,128]{2,1,0:T(8,128)(2,1)S(1)}, u32[]{:S(2)}, u32[]{:S(2)}) async-start(bf16[16,272,128]{2,1,0:T(8,128)(2,1)} %prefix.1), calls=%async_computation.4 | async-start | bytes 2228224 | tf_op jit(solution)/shard_map/prefix/all_to_all | solution.py:128
  91.0 1.7 copy-start.4
  91.1 2.3 %copy-start.3 = (bf16[4,256,512]{2,1,0:T(8,128)(2,1)S(1)}, bf16[4,256,512]{2,1,0:T(8,128)(2,1)}, u32[]{:S(2)}) copy-start(bf16[4,256,512]{2,1,0:T(8,128)(2,1)} %get-tuple-element.14) | copy-start | bytes 3145732
  107.2 40.6 %copy-start.2 = (bf16[16,40,1024]{2,1,0:T(8,128)(2,1)S(1)}, bf16[16,40,1024]{2,1,0:T(8,128)(2,1)}, u32[]{:S(2)}) copy-start(bf16[16,40,1024]{2,1,0:T(8,128)(2,1)} %copy-done.1) | copy-start | bytes 3932164

commit v5 on v4

--- a/solution.py
+++ b/solution.py
@@ -53,12 +53,9 @@
         out_ref[at * per : (at + 1) * per, pl.ds(pl.multiple_of(head * rows, rows), rows), :] = (
             (both[:, :HD] / summed).astype(BF16).reshape(per, rows, HD)
         )
-        lse = top * FACTOR + jnp.log(summed)
-        for j in range(TILE // 128):
-            lse_ref[
-                pl.ds(pl.multiple_of(head * 8, 8), 8),
-                at * TILE + 128 * j : at * TILE + 128 * j + 128,
-            ] = lse[128 * j : 128 * j + 128].T[0:8]
+        lse_ref[pl.ds(pl.multiple_of(head * 8, 8), 8), at * TILE : (at + 1) * TILE] = (
+            jnp.broadcast_to(top, (TILE, HD)).T[0:8] * FACTOR + jnp.log(summed.T[0:8])
+        )
 
     @pl.when(head == KVH - 1)
     def _():
@@ -148,7 +145,8 @@
         payload = jnp.concatenate([asked, w_out.T.reshape(GROUP, width, HD)], axis=1)
         payload = a2a(payload, "ctx", near)
         asked = payload[:, : share * rows]
-        block = payload[:, share * rows :].transpose(1, 0, 2).reshape(width, GROUP * HD)
+        block = payload[:, share * rows :].reshape(GROUP // 2, 2, width, HD)
+        block = block.transpose(2, 1, 0, 3).reshape(width, GROUP * HD)
 
     with jax.named_scope("weights"):
         weights = a2a(jnp.broadcast_to(block[None], (req, *block.shape)), "req")
@@ -221,15 +219,20 @@
         attention = attention.astype(BF16)
 
     with jax.named_scope("projection"):
-        shared = a2a(jnp.broadcast_to(attention[None], (GROUP, *attention.shape)), "ctx", near)
+        quads = [list(range(a + core, a + GROUP, 2)) for a in range(0, ctx, GROUP) for core in (0, 1)]
+        pairs = [[a, a + 1] for a in range(0, ctx, 2)]
+        half = GROUP // 2
+        shared = a2a(jnp.broadcast_to(attention[None], (half, *attention.shape)), "ctx", quads)
+        shared = lax.all_gather(shared, "ctx", axis=0, tiled=True, axis_index_groups=pairs)
         shared = shared.transpose(1, 0, 2).reshape(group_rows, GROUP * HD)
         terms = lax.dot_general(
             shared, weights, (((1,), (1,)), ((), ())), preferred_element_type=F32
         ).astype(BF16)
         home = a2a(terms.reshape(ctx, rows, -1), "ctx")
-        home = home.reshape(ctx // GROUP, GROUP, rows, req, width).astype(F32)
-        summed = jnp.sum(home, axis=0).transpose(1, 2, 0, 3)
-        return summed.reshape(rows, -1).astype(BF16)
+        home = home.reshape(ctx // GROUP, GROUP, rows, req * width).astype(F32)
+        summed = lax.optimization_barrier(jnp.sum(home, axis=0).astype(BF16))
+        summed = summed.reshape(GROUP, rows, req, width).transpose(1, 2, 0, 3)
+        return summed.reshape(rows, -1)
 
 
 def solution(mesh):

time: 173 us -> 171 us (0.988)
  blocking collectives: 108 us -> 106 us
    all_to_all x5, blocking collectives: 86.8 us -> 80.9 us  [a2a(): return lax.all_to_all(x, axis, 0, 0, tiled=True, axis_index_groups=groups)]
    all_gather x0 -> x1, blocking collectives: none -> 4.37 us  [local(): lax.all_gather(shared, 'ctx', axis=0, tiled=True, axis_index_groups=pairs)]
    convert_element_type x4 -> x0, local copies, waits for them, and re-layouts: 1.8 us -> none  [the longest x2 0.91 us: local(): return summed.reshape(rows, -1).astype(BF16)]
where the time goes in v5:
time: 171 us; the launch traced here: 170 us
  blocking collectives  106 us (62%)
  waiting for transfers between devices  23.7 us (14%)
  starting transfers between devices  16.7 us (10%)
  local copies, waits for them, and re-layouts  10.4 us (6%)
  Pallas kernels  8.05 us (5%)
  other arithmetic  2.69 us (2%)
  matrix products  1.71 us (1%)
    all_to_all x5, blocking collectives, a2a(): return lax.all_to_all(x, axis, 0, 0, tiled=True, axis_index_groups=groups)  80.9 us
    all_to_all x3, waiting for transfers between devices, a2a(): return lax.all_to_all(x, axis, 0, 0, tiled=True, axis_index_groups=groups)  23.7 us
    all_gather x1, blocking collectives, local(): lax.all_gather(asked, 'ctx', axis=0, tiled=True, axis_index_groups=far)  21 us
    all_to_all x3, starting transfers between devices, a2a(): return lax.all_to_all(x, axis, 0, 0, tiled=True, axis_index_groups=groups)  16.7 us
    pallas_call x1, Pallas kernels, prefix_attention(): pl.pallas_call(attention_kernel, out_shape=jax.ShapeDtypeStruct((groups,...  8.05 us
    all_gather x1, blocking collectives, local(): lax.all_gather(shared, 'ctx', axis=0, tiled=True, axis_index_groups=pairs)  4.37 us
  transfers between devices with their start and end apart: 3, of which 2 were waited for; matrix products, arithmetic and copies ran while one was open for 4% of the time, Pallas kernels for 0%

profile of v5, /device:TPU:1, one launch (start us, length us, event | category | flops | bytes accessed | tf_op | source)
XLA Modules:
  0.0 169.9 jit_solution(16500938514891619431)
XLA Ops:
  0.0 0.9 pad_maximum_fusion
  0.9 15.0 %all_to_all.40 = bf16[8,56,128]{2,1,0:T(8,128)(2,1)S(1)} all-to-all(bf16[8,56,128]{2,1,0:T(8,128)(2,1)S(1)} %pad_maximum_fusion), channel_id=1, replica_groups={{0,1,2,3,4,5,6,7},{8,9,10,11,12,13,14,15},{16,17,18,19,20,21,22,23},{24..., dimensions={0} | all-to-all | bytes 229376 | tf_op jit(solution)/shard_map/split_near/all_to_all | solution.py:125
  16.0 1.2 broadcast_in_dim.41
  17.2 4.8 %all-to-all-start.1 = ((bf16[16,40,1024]{2,1,0:T(8,128)(2,1)}), bf16[16,40,1024]{2,1,0:T(8,128)(2,1)S(1)}, u32[]{:S(2)}, u32[]{:S(2)}) async-start(bf16[16,40,1024]{2,1,0:T(8,128)(2,1)} %broadcast_in_dim.41), calls=%async_computation.1 | async-start | bytes 2621440 | tf_op jit(solution)/shard_map/weights/all_to_all | solution.py:125
  22.3 21.0 %all_gather.6 = bf16[32,16,128]{2,1,0:T(8,128)(2,1)S(1)} all-gather(bf16[8,16,128]{2,1,0:T(8,128)(2,1)S(1)} %slice.44), channel_id=1, replica_groups={{0,8,16,24},{1,9,17,25},{2,10,18,26},{3,11,19,27},{4,12,20,28},{5,13,21..., dimensions={0}, use_global_device_ids=true | all-gather | bytes 163840 | tf_op jit(solution)/shard_map/gather_far/all_gather | solution.py:156
  43.6 11.0 %all_to_all.41 = bf16[8,4,8,128]{3,2,1,0:T(8,128)(2,1)S(1)} all-to-all(bf16[8,4,8,128]{3,2,1,0:T(8,128)(2,1)S(1)} %fusion.1), channel_id=1, replica_groups={{0,1,2,3,4,5,6,7},{8,9,10,11,12,13,14,15},{16,17,18,19,20,21,22,23},{24..., dimensions={0} | all-to-all | bytes 131072 | tf_op jit(solution)/shard_map/slots/all_to_all | solution.py:125
  54.7 1.2 broadcast_in_dim.43
  55.9 7.8 %all-to-all-start.3 = ((bf16[16,256,128]{2,1,0:T(8,128)(2,1)}), bf16[16,256,128]{2,1,0:T(8,128)(2,1)S(1)}, u32[]{:S(2)}, u32[]{:S(2)}) async-start(bf16[16,256,128]{2,1,0:T(8,128)(2,1)} %broadcast_in_dim.43), calls=%async_computation.3 | async-start | bytes 2097152 | tf_op jit(solution)/shard_map/gather_req/all_to_all | solution.py:125
  63.7 3.1 %fusion.34 = (bf16[4,256,512]{2,1,0:T(8,128)(2,1)}, bf16[4,256,512]{2,1,0:T(8,128)(2,1)}) fusion(bf16[4,256,1024]{2,1,0:T(8,128)(2,1)} %param.10), kind=kLoop, calls=%fused_computation.65 | loop fusion | bytes 4194304 | tf_op jit(solution)/shard_map/suffix/slice | solution.py:109
  66.8 12.2 %all-to-all-done.3.q_ref = bf16[16,256,128]{2,1,0:T(8,128)(2,1)S(1)} async-done(((bf16[16,256,128]{2,1,0:T(8,128)(2,1)}), bf16[16,256,128]{2,1,0:T(8,128)(2,1)S(1)}, u32[]{:S(2)}, u32[]{:S(2)}) %all-to-all-start.3) | async-done | bytes 1048608 | tf_op jit(solution)/shard_map/gather_req/all_to_all | solution.py:125
  79.0 8.0 %prefix.1 = bf16[16,272,128]{2,1,0:T(8,128)(2,1)} custom-call(bf16[16,256,128]{2,1,0:T(8,128)(2,1)S(1)} %all-to-all-done.3.q_ref, bf16[1024,1024]{1,0:T(8,128)(2,1)S(1)} %bitcast.72, bf16[1024,1024]{1,0:T(8,128)(2,1)S(1)} %bitcast.73), custom_call_target="tpu_custom_call" | custom-call | flops 2147483648 | bytes 4194304 | tf_op jit(solution)/shard_map/prefix/pallas_call | solution.py:84
  87.1 4.1 %all-to-all-start.4 = ((bf16[16,272,128]{2,1,0:T(8,128)(2,1)}), bf16[16,272,128]{2,1,0:T(8,128)(2,1)S(1)}, u32[]{:S(2)}, u32[]{:S(2)}) async-start(bf16[16,272,128]{2,1,0:T(8,128)(2,1)} %prefix.1), calls=%async_computation.4 | async-start | bytes 2228224 | tf_op jit(solution)/shard_map/prefix/all_to_all | solution.py:125
  91.2 1.6 copy.148
  92.8 0.3 fusion.35
  93.5 0.5 copy.149
  94.0 0.4 fusion.6
  94.5 11.6 %all-to-all-done.4 = bf16[16,272,128]{2,1,0:T(8,128)(2,1)S(1)} async-done(((bf16[16,272,128]{2,1,0:T(8,128)(2,1)}), bf16[16,272,128]{2,1,0:T(8,128)(2,1)S(1)}, u32[]{:S(2)}, u32[]{:S(2)}) %all-to-all-start.4) | async-done | bytes 1114144 | tf_op jit(solution)/shard_map/prefix/all_to_all | solution.py:125
  106.6 0.7 multiply_reduce_fusion
  107.7 26.4 %all_to_all.42 = bf16[32,16,128]{2,1,0:T(8,128)(2,1)S(1)} all-to-all(bf16[32,16,128]{2,1,0:T(8,128)(2,1)S(1)} %maximum_maximum_fusion), channel_id=1, replica_groups=mesh['req'=16,'ctx'=32] {'ctx'}, dimensions={0} | all-to-all | bytes 262144 | tf_op jit(solution)/shard_map/to_heads/all_to_all | solution.py:125
  135.1 7.2 %all_to_all.43 = bf16[4,128,128]{2,1,0:T(8,128)(2,1)S(1)} all-to-all(bf16[4,128,128]{2,1,0:T(8,128)(2,1)S(1)} %broadcast_in_dim.80), channel_id=1, replica_groups={{0,2,4,6},{1,3,5,7},{8,10,12,14},{9,11,13,15},{16,18,20,22},{17,19,21,2..., dimensions={0} | all-to-all | bytes 262144 | tf_op jit(solution)/shard_map/projection/all_to_all | solution.py:125
  142.3 4.4 %all_gather.7 = bf16[8,128,128]{2,1,0:T(8,128)(2,1)S(1)} all-gather(bf16[4,128,128]{2,1,0:T(8,128)(2,1)S(1)} %all_to_all.43), channel_id=1, replica_groups={{0,1},{2,3},{4,5},{6,7},{8,9},{10,11},{12,13},{14,15},{16,17},{18,19},{..., dimensions={0}, use_global_device_ids=true | all-gather | bytes 393216 | tf_op jit(solution)/shard_map/projection/all_gather | solution.py:226
  146.8 0.5 convolution_convert_fusion
  147.4 21.3 %all_to_all.44 = bf16[32,4,640]{2,1,0:T(4,128)(2,1)S(1)} all-to-all(bf16[32,4,640]{2,1,0:T(4,128)(2,1)S(1)} %reshape.203), channel_id=1, replica_groups=mesh['req'=16,'ctx'=32] {'ctx'}, dimensions={0} | all-to-all | bytes 327680 | tf_op jit(solution)/shard_map/projection/all_to_all | solution.py:125
  169.1 0.8 reshape.206
  (70 shorter events, 3.4 us)
Async XLA Ops:
  17.2 4.9 %copy-start.5 = (s32[128]{0:T(128)S(1)}, s32[128]{0:T(128)}, u32[]{:S(2)}) copy-start(s32[128]{0:T(128)} %param.7) | copy-start | bytes 1540
  17.2 26.4 %all-to-all-start.1 = ((bf16[16,40,1024]{2,1,0:T(8,128)(2,1)}), bf16[16,40,1024]{2,1,0:T(8,128)(2,1)S(1)}, u32[]{:S(2)}, u32[]{:S(2)}) async-start(bf16[16,40,1024]{2,1,0:T(8,128)(2,1)} %broadcast_in_dim.41), calls=%async_computation.1 | async-start | bytes 2621440 | tf_op jit(solution)/shard_map/weights/all_to_all | solution.py:125
  43.6 12.2 %copy-start.1 = (bf16[16,40,1024]{2,1,0:T(8,128)(2,1)}, bf16[16,40,1024]{2,1,0:T(8,128)(2,1)S(1)}, u32[]{:S(2)}) copy-start(bf16[16,40,1024]{2,1,0:T(8,128)(2,1)S(1)} %all-to-all-done.1) | copy-start | bytes 3932164
  55.9 23.2 %all-to-all-start.3 = ((bf16[16,256,128]{2,1,0:T(8,128)(2,1)}), bf16[16,256,128]{2,1,0:T(8,128)(2,1)S(1)}, u32[]{:S(2)}, u32[]{:S(2)}) async-start(bf16[16,256,128]{2,1,0:T(8,128)(2,1)} %broadcast_in_dim.43), calls=%async_computation.3 | async-start | bytes 2097152 | tf_op jit(solution)/shard_map/gather_req/all_to_all | solution.py:125
  63.7 15.3 %copy-start = (bf16[1,1024,1024]{2,1,0:T(8,128)(2,1)S(1)}, bf16[1,1024,1024]{2,1,0:T(8,128)(2,1)}, u32[]{:S(2)}) copy-start(bf16[1,1024,1024]{2,1,0:T(8,128)(2,1)} %param.9) | copy-start | bytes 6291460
  87.1 4.1 %copy-start.6 = (s32[1,4]{1,0:T(1,128)S(1)}, s32[1,4]{1,0:T(1,128)}, u32[]{:S(2)}) copy-start(s32[1,4]{1,0:T(1,128)} %param.8) | copy-start | bytes 52
  87.1 19.0 %all-to-all-start.4 = ((bf16[16,272,128]{2,1,0:T(8,128)(2,1)}), bf16[16,272,128]{2,1,0:T(8,128)(2,1)S(1)}, u32[]{:S(2)}, u32[]{:S(2)}) async-start(bf16[16,272,128]{2,1,0:T(8,128)(2,1)} %prefix.1), calls=%async_computation.4 | async-start | bytes 2228224 | tf_op jit(solution)/shard_map/prefix/all_to_all | solution.py:125
  91.2 1.7 copy-start.4
  91.2 2.3 %copy-start.3 = (bf16[4,256,512]{2,1,0:T(8,128)(2,1)S(1)}, bf16[4,256,512]{2,1,0:T(8,128)(2,1)}, u32[]{:S(2)}) copy-start(bf16[4,256,512]{2,1,0:T(8,128)(2,1)} %get-tuple-element.14) | copy-start | bytes 3145732
  107.6 39.2 %copy-start.2 = (bf16[16,40,1024]{2,1,0:T(8,128)(2,1)S(1)}, bf16[16,40,1024]{2,1,0:T(8,128)(2,1)}, u32[]{:S(2)}) copy-start(bf16[16,40,1024]{2,1,0:T(8,128)(2,1)} %copy-done.1) | copy-start | bytes 3932164

commit v6 on v5

--- a/solution.py
+++ b/solution.py
@@ -27,78 +27,88 @@
     return high.astype(BF16), middle.astype(BF16), (rest - middle).astype(BF16)
 
 
-def attention_kernel(q_ref, k_ref, v_ref, out_ref, lse_ref):
-    head = pl.program_id(0)
-    groups, rows, _ = q_ref.shape
+def attention_kernel(q_ref, kv_ref, out_ref, held, lse_ref, sems):
+    groups, all_rows, _ = q_ref.shape
+    rows = all_rows // KVH
     total = groups * rows
-    keys = k_ref[...]
-    values = jnp.concatenate([v_ref[...], jnp.ones((v_ref.shape[0], HD), BF16)], axis=1)
     per = TILE // rows
-
-    def score(at):
-        queries = q_ref[at * per : (at + 1) * per].reshape(TILE, HD)
-        return lax.dot_general(
-            queries, keys, (((1,), (1,)), ((), ())), preferred_element_type=F32
-        )
-
-    following = score(0)
-    for at in range(total // TILE):
-        scores = following
-        if (at + 1) * TILE < total:
-            following = score(at + 1)
-        top = jnp.max(scores, axis=1, keepdims=True)
-        weights = jnp.exp2((scores - top) * (FACTOR * LOG2E)).astype(BF16)
-        both = jnp.dot(weights, values, preferred_element_type=F32)
-        summed = both[:, HD:]
-        out_ref[at * per : (at + 1) * per, pl.ds(pl.multiple_of(head * rows, rows), rows), :] = (
-            (both[:, :HD] / summed).astype(BF16).reshape(per, rows, HD)
-        )
-        lse_ref[pl.ds(pl.multiple_of(head * 8, 8), 8), at * TILE : (at + 1) * TILE] = (
-            jnp.broadcast_to(top, (TILE, HD)).T[0:8] * FACTOR + jnp.log(summed.T[0:8])
-        )
-
-    @pl.when(head == KVH - 1)
-    def _():
-        row = lax.broadcasted_iota(jnp.int32, (8, total), 0)
-        upper = jnp.zeros((8, total), F32)
-        lower = upper
-        for h in range(KVH):
-            whole = lse_ref[8 * h : 8 * h + 8, :]
-            high = whole.astype(BF16).astype(F32)
-            rest = whole - high
-            middle = rest.astype(BF16).astype(F32)
-            upper = jnp.where(row == h, high, jnp.where(row == KVH + h, middle, upper))
-            lower = jnp.where(row == h, rest - middle, lower)
-        parts = jnp.concatenate([upper, lower], axis=0)
-        rolled = pltpu.roll(parts, total - rows, 1)
-        for r in range(groups):
-            source = parts if r % 2 == 0 else rolled
-            at = r // 2 * 128
-            out_ref[r, KVH * rows :, :] = source[:, at : at + 128].astype(BF16)
+    copies = []
+
+    def leave(first, count):
+        at = (slice(None), slice(first, first + count))
+        copies.append(pltpu.make_async_copy(held.at[at], out_ref.at[at], sems.at[len(copies)]))
+        copies[-1].start()
+
+    for head in range(KVH):
+        keys = kv_ref[:, head * HD : (head + 1) * HD]
+        values = kv_ref[:, (KVH + head) * HD : (KVH + head + 1) * HD]
+        values = jnp.concatenate([values, jnp.ones_like(values)], axis=1)
+        first = head * rows
+
+        def score(at):
+            queries = q_ref[at * per : (at + 1) * per, first : first + rows].reshape(TILE, HD)
+            return lax.dot_general(
+                queries, keys, (((1,), (1,)), ((), ())), preferred_element_type=F32
+            )
+
+        following = score(0)
+        for at in range(total // TILE):
+            scores = following
+            if (at + 1) * TILE < total:
+                following = score(at + 1)
+            top = jnp.max(scores, axis=1, keepdims=True)
+            weights = jnp.exp2((scores - top) * (FACTOR * LOG2E)).astype(BF16)
+            both = jnp.dot(weights, values, preferred_element_type=F32)
+            summed = both[:, HD:]
+            held[at * per : (at + 1) * per, first : first + rows] = (
+                (both[:, :HD] / summed).astype(BF16).reshape(per, rows, HD)
+            )
+            lse_ref[head * 8 : head * 8 + 8, at * TILE : (at + 1) * TILE] = (
+                jnp.broadcast_to(top, (TILE, HD)).T[0:8] * FACTOR + jnp.log(summed.T[0:8])
+            )
+        leave(first, rows)
+
+    row = lax.broadcasted_iota(jnp.int32, (8, total), 0)
+    upper = jnp.zeros((8, total), F32)
+    lower = upper
+    for h in range(KVH):
+        whole = lse_ref[8 * h : 8 * h + 8, :]
+        high = whole.astype(BF16).astype(F32)
+        rest = whole - high
+        middle = rest.astype(BF16).astype(F32)
+        upper = jnp.where(row == h, high, jnp.where(row == KVH + h, middle, upper))
+        lower = jnp.where(row == h, rest - middle, lower)
+    parts = jnp.concatenate([upper, lower], axis=0)
+    rolled = pltpu.roll(parts, total - rows, 1)
+    for r in range(groups):
+        source = parts if r % 2 == 0 else rolled
+        at = r // 2 * 128
+        held[r, all_rows:] = source[:, at : at + 128].astype(BF16)
+    leave(all_rows, 16)
+    for copy in copies:
+        copy.wait()
 
 
 def prefix_attention(queries, kv):
     groups, rows, _ = queries.shape
     tokens = kv.shape[0]
-    each = rows // KVH
     return pl.pallas_call(
         attention_kernel,
         out_shape=jax.ShapeDtypeStruct((groups, rows + 16, HD), BF16),
-        grid=(KVH,),
-        in_specs=[
-            pl.BlockSpec((groups, each, HD), lambda h: (0, h, 0)),
-            pl.BlockSpec((tokens, HD), lambda h: (0, h)),
-            pl.BlockSpec((tokens, HD), lambda h: (0, KVH + h)),
+        in_specs=[pl.BlockSpec(memory_space=pltpu.VMEM)] * 2,
+        out_specs=pl.BlockSpec(memory_space=pl.ANY),
+        scratch_shapes=[
+            pltpu.VMEM((groups, rows + 16, HD), BF16),
+            pltpu.VMEM((8 * KVH, groups * rows // KVH), F32),
+            pltpu.SemaphoreType.DMA((KVH + 1,)),
         ],
-        out_specs=pl.BlockSpec((groups, rows + 16, HD), lambda h: (0, 0, 0)),
-        scratch_shapes=[pltpu.VMEM((8 * KVH, groups * each), F32)],
-        compiler_params=pltpu.CompilerParams(vmem_limit_bytes=48 * 2**20),
+        compiler_params=pltpu.CompilerParams(vmem_limit_bytes=40 * 2**20),
         cost_estimate=pl.CostEstimate(
             flops=4 * groups * rows * tokens * HD,
             bytes_accessed=4 * groups * rows * HD + 4 * tokens * KVH * HD,
             transcendentals=groups * rows * tokens,
         ),
-    )(queries, kv, kv)
+    )(queries, kv)
 
 
 def suffix_attention(query, suffix_kv, lengths):

time: 171 us -> 169 us (0.988)
  no operation moved by 1% of the time
where the time goes in v6:
time: 169 us
  blocking collectives  106 us (63%)
  waiting for transfers between devices  23.7 us (14%)
  starting transfers between devices  16.6 us (10%)
  local copies, waits for them, and re-layouts  10.4 us (6%)
  Pallas kernels  6.77 us (4%)
  other arithmetic  2.69 us (2%)
  matrix products  1.71 us (1%)
    all_to_all x5, blocking collectives, a2a(): return lax.all_to_all(x, axis, 0, 0, tiled=True, axis_index_groups=groups)  80.9 us
    all_to_all x3, waiting for transfers between devices, a2a(): return lax.all_to_all(x, axis, 0, 0, tiled=True, axis_index_groups=groups)  23.7 us
    all_gather x1, blocking collectives, local(): lax.all_gather(asked, 'ctx', axis=0, tiled=True, axis_index_groups=far)  21 us
    all_to_all x3, starting transfers between devices, a2a(): return lax.all_to_all(x, axis, 0, 0, tiled=True, axis_index_groups=groups)  16.6 us
    pallas_call x1, Pallas kernels, prefix_attention(): pl.pallas_call(attention_kernel, out_shape=jax.ShapeDtypeStruct((groups,...  6.77 us
    all_gather x1, blocking collectives, local(): lax.all_gather(shared, 'ctx', axis=0, tiled=True, axis_index_groups=pairs)  4.37 us
  transfers between devices with their start and end apart: 3, of which 2 were waited for; matrix products, arithmetic and copies ran while one was open for 4% of the time, Pallas kernels for 0%

profile of v6, /device:TPU:1, one launch (start us, length us, event | category | flops | bytes accessed | tf_op | source)
XLA Modules:
  0.0 168.6 jit_solution(18031118613459375241)
XLA Ops:
  0.0 0.9 pad_maximum_fusion
  0.9 15.0 %all_to_all.40 = bf16[8,56,128]{2,1,0:T(8,128)(2,1)S(1)} all-to-all(bf16[8,56,128]{2,1,0:T(8,128)(2,1)S(1)} %pad_maximum_fusion), channel_id=1, replica_groups={{0,1,2,3,4,5,6,7},{8,9,10,11,12,13,14,15},{16,17,18,19,20,21,22,23},{24..., dimensions={0} | all-to-all | bytes 229376 | tf_op jit(solution)/shard_map/split_near/all_to_all | solution.py:135
  16.0 1.2 broadcast_in_dim.41
  17.2 4.8 %all-to-all-start.1 = ((bf16[16,40,1024]{2,1,0:T(8,128)(2,1)}), bf16[16,40,1024]{2,1,0:T(8,128)(2,1)S(1)}, u32[]{:S(2)}, u32[]{:S(2)}) async-start(bf16[16,40,1024]{2,1,0:T(8,128)(2,1)} %broadcast_in_dim.41), calls=%async_computation.1 | async-start | bytes 2621440 | tf_op jit(solution)/shard_map/weights/all_to_all | solution.py:135
  22.3 21.0 %all_gather.6 = bf16[32,16,128]{2,1,0:T(8,128)(2,1)S(1)} all-gather(bf16[8,16,128]{2,1,0:T(8,128)(2,1)S(1)} %slice.44), channel_id=1, replica_groups={{0,8,16,24},{1,9,17,25},{2,10,18,26},{3,11,19,27},{4,12,20,28},{5,13,21..., dimensions={0}, use_global_device_ids=true | all-gather | bytes 163840 | tf_op jit(solution)/shard_map/gather_far/all_gather | solution.py:166
  43.6 11.0 %all_to_all.41 = bf16[8,4,8,128]{3,2,1,0:T(8,128)(2,1)S(1)} all-to-all(bf16[8,4,8,128]{3,2,1,0:T(8,128)(2,1)S(1)} %fusion.1), channel_id=1, replica_groups={{0,1,2,3,4,5,6,7},{8,9,10,11,12,13,14,15},{16,17,18,19,20,21,22,23},{24..., dimensions={0} | all-to-all | bytes 131072 | tf_op jit(solution)/shard_map/slots/all_to_all | solution.py:135
  54.7 1.2 broadcast_in_dim.43
  55.9 7.8 %all-to-all-start.3 = ((bf16[16,256,128]{2,1,0:T(8,128)(2,1)}), bf16[16,256,128]{2,1,0:T(8,128)(2,1)S(1)}, u32[]{:S(2)}, u32[]{:S(2)}) async-start(bf16[16,256,128]{2,1,0:T(8,128)(2,1)} %broadcast_in_dim.43), calls=%async_computation.3 | async-start | bytes 2097152 | tf_op jit(solution)/shard_map/gather_req/all_to_all | solution.py:135
  63.7 3.1 %fusion.34 = (bf16[4,256,512]{2,1,0:T(8,128)(2,1)}, bf16[4,256,512]{2,1,0:T(8,128)(2,1)}) fusion(bf16[4,256,1024]{2,1,0:T(8,128)(2,1)} %param.10), kind=kLoop, calls=%fused_computation.65 | loop fusion | bytes 4194304 | tf_op jit(solution)/shard_map/suffix/slice | solution.py:119
  66.8 12.2 %all-to-all-done.3.q_ref = bf16[16,256,128]{2,1,0:T(8,128)(2,1)S(1)} async-done(((bf16[16,256,128]{2,1,0:T(8,128)(2,1)}), bf16[16,256,128]{2,1,0:T(8,128)(2,1)S(1)}, u32[]{:S(2)}, u32[]{:S(2)}) %all-to-all-start.3) | async-done | bytes 1048608 | tf_op jit(solution)/shard_map/gather_req/all_to_all | solution.py:135
  79.0 6.8 %prefix.1 = bf16[16,272,128]{2,1,0:T(8,128)(2,1)} custom-call(bf16[16,256,128]{2,1,0:T(8,128)(2,1)S(1)} %all-to-all-done.3.q_ref, bf16[1024,1024]{1,0:T(8,128)(2,1)S(1)} %bitcast.72), custom_call_target="tpu_custom_call" | custom-call | flops 2147483648 | bytes 4194304 | tf_op jit(solution)/shard_map/prefix/pallas_call | solution.py:95
  85.8 3.9 %all-to-all-start.4 = ((bf16[16,272,128]{2,1,0:T(8,128)(2,1)}), bf16[16,272,128]{2,1,0:T(8,128)(2,1)S(1)}, u32[]{:S(2)}, u32[]{:S(2)}) async-start(bf16[16,272,128]{2,1,0:T(8,128)(2,1)} %prefix.1), calls=%async_computation.4 | async-start | bytes 2228224 | tf_op jit(solution)/shard_map/prefix/all_to_all | solution.py:135
  89.8 1.6 copy.148
  91.5 0.3 fusion.35
  92.1 0.5 copy.149
  92.6 0.4 fusion.6
  93.2 11.6 %all-to-all-done.4 = bf16[16,272,128]{2,1,0:T(8,128)(2,1)S(1)} async-done(((bf16[16,272,128]{2,1,0:T(8,128)(2,1)}), bf16[16,272,128]{2,1,0:T(8,128)(2,1)S(1)}, u32[]{:S(2)}, u32[]{:S(2)}) %all-to-all-start.4) | async-done | bytes 1114144 | tf_op jit(solution)/shard_map/prefix/all_to_all | solution.py:135
  105.2 0.7 multiply_reduce_fusion
  106.3 26.4 %all_to_all.42 = bf16[32,16,128]{2,1,0:T(8,128)(2,1)S(1)} all-to-all(bf16[32,16,128]{2,1,0:T(8,128)(2,1)S(1)} %maximum_maximum_fusion), channel_id=1, replica_groups=mesh['req'=16,'ctx'=32] {'ctx'}, dimensions={0} | all-to-all | bytes 262144 | tf_op jit(solution)/shard_map/to_heads/all_to_all | solution.py:135
  133.7 7.2 %all_to_all.43 = bf16[4,128,128]{2,1,0:T(8,128)(2,1)S(1)} all-to-all(bf16[4,128,128]{2,1,0:T(8,128)(2,1)S(1)} %broadcast_in_dim.80), channel_id=1, replica_groups={{0,2,4,6},{1,3,5,7},{8,10,12,14},{9,11,13,15},{16,18,20,22},{17,19,21,2..., dimensions={0} | all-to-all | bytes 262144 | tf_op jit(solution)/shard_map/projection/all_to_all | solution.py:135
  140.9 4.4 %all_gather.7 = bf16[8,128,128]{2,1,0:T(8,128)(2,1)S(1)} all-gather(bf16[4,128,128]{2,1,0:T(8,128)(2,1)S(1)} %all_to_all.43), channel_id=1, replica_groups={{0,1},{2,3},{4,5},{6,7},{8,9},{10,11},{12,13},{14,15},{16,17},{18,19},{..., dimensions={0}, use_global_device_ids=true | all-gather | bytes 393216 | tf_op jit(solution)/shard_map/projection/all_gather | solution.py:236
  145.5 0.5 convolution_convert_fusion
  146.1 21.3 %all_to_all.44 = bf16[32,4,640]{2,1,0:T(4,128)(2,1)S(1)} all-to-all(bf16[32,4,640]{2,1,0:T(4,128)(2,1)S(1)} %reshape.203), channel_id=1, replica_groups=mesh['req'=16,'ctx'=32] {'ctx'}, dimensions={0} | all-to-all | bytes 327680 | tf_op jit(solution)/shard_map/projection/all_to_all | solution.py:135
  167.7 0.8 reshape.206
  (70 shorter events, 3.4 us)
Async XLA Ops:
  17.2 4.9 %copy-start.5 = (s32[128]{0:T(128)S(1)}, s32[128]{0:T(128)}, u32[]{:S(2)}) copy-start(s32[128]{0:T(128)} %param.7) | copy-start | bytes 1540
  17.2 26.4 %all-to-all-start.1 = ((bf16[16,40,1024]{2,1,0:T(8,128)(2,1)}), bf16[16,40,1024]{2,1,0:T(8,128)(2,1)S(1)}, u32[]{:S(2)}, u32[]{:S(2)}) async-start(bf16[16,40,1024]{2,1,0:T(8,128)(2,1)} %broadcast_in_dim.41), calls=%async_computation.1 | async-start | bytes 2621440 | tf_op jit(solution)/shard_map/weights/all_to_all | solution.py:135
  43.6 12.2 %copy-start.1 = (bf16[16,40,1024]{2,1,0:T(8,128)(2,1)}, bf16[16,40,1024]{2,1,0:T(8,128)(2,1)S(1)}, u32[]{:S(2)}) copy-start(bf16[16,40,1024]{2,1,0:T(8,128)(2,1)S(1)} %all-to-all-done.1) | copy-start | bytes 3932164
  55.9 23.2 %all-to-all-start.3 = ((bf16[16,256,128]{2,1,0:T(8,128)(2,1)}), bf16[16,256,128]{2,1,0:T(8,128)(2,1)S(1)}, u32[]{:S(2)}, u32[]{:S(2)}) async-start(bf16[16,256,128]{2,1,0:T(8,128)(2,1)} %broadcast_in_dim.43), calls=%async_computation.3 | async-start | bytes 2097152 | tf_op jit(solution)/shard_map/gather_req/all_to_all | solution.py:135
  63.7 15.3 %copy-start = (bf16[1,1024,1024]{2,1,0:T(8,128)(2,1)S(1)}, bf16[1,1024,1024]{2,1,0:T(8,128)(2,1)}, u32[]{:S(2)}) copy-start(bf16[1,1024,1024]{2,1,0:T(8,128)(2,1)} %param.9) | copy-start | bytes 6291460
  85.8 4.0 %copy-start.6 = (s32[1,4]{1,0:T(1,128)S(1)}, s32[1,4]{1,0:T(1,128)}, u32[]{:S(2)}) copy-start(s32[1,4]{1,0:T(1,128)} %param.8) | copy-start | bytes 52
  85.8 18.9 %all-to-all-start.4 = ((bf16[16,272,128]{2,1,0:T(8,128)(2,1)}), bf16[16,272,128]{2,1,0:T(8,128)(2,1)S(1)}, u32[]{:S(2)}, u32[]{:S(2)}) async-start(bf16[16,272,128]{2,1,0:T(8,128)(2,1)} %prefix.1), calls=%async_computation.4 | async-start | bytes 2228224 | tf_op jit(solution)/shard_map/prefix/all_to_all | solution.py:135
  89.8 1.7 copy-start.4
  89.8 2.3 %copy-start.3 = (bf16[4,256,512]{2,1,0:T(8,128)(2,1)S(1)}, bf16[4,256,512]{2,1,0:T(8,128)(2,1)}, u32[]{:S(2)}) copy-start(bf16[4,256,512]{2,1,0:T(8,128)(2,1)} %get-tuple-element.14) | copy-start | bytes 3145732
  106.2 39.2 %copy-start.2 = (bf16[16,40,1024]{2,1,0:T(8,128)(2,1)S(1)}, bf16[16,40,1024]{2,1,0:T(8,128)(2,1)}, u32[]{:S(2)}) copy-start(bf16[16,40,1024]{2,1,0:T(8,128)(2,1)} %copy-done.1) | copy-start | bytes 3932164

commit v7 on v6

--- a/solution.py
+++ b/solution.py
@@ -198,8 +198,9 @@
         peak = jnp.max(logs, axis=0)
         shares = jnp.exp(logs - peak)
         total = jnp.sum(shares, axis=0)
+        shares = shares / total
         merged = jnp.sum(shares[..., None] * received[:, :count].astype(F32), axis=0)
-        merged = (merged / total[:, None]).astype(BF16)
+        merged = merged.astype(BF16)
         merged_lse = (peak + jnp.log(total)).reshape(heads, SLOTS)
 
     with jax.named_scope("to_heads"):

time: 169 us -> 169 us (level)
  no operation moved by 1% of the time
where the time goes in v7:
time: 169 us; the launch traced here: 168 us
  blocking collectives  106 us (63%)
  waiting for transfers between devices  23.7 us (14%)
  starting transfers between devices  16.6 us (10%)
  local copies, waits for them, and re-layouts  10.2 us (6%)
  Pallas kernels  6.77 us (4%)
  other arithmetic  2.6 us (2%)
  matrix products  1.71 us (1%)
    all_to_all x5, blocking collectives, a2a(): return lax.all_to_all(x, axis, 0, 0, tiled=True, axis_index_groups=groups)  80.9 us
    all_to_all x3, waiting for transfers between devices, a2a(): return lax.all_to_all(x, axis, 0, 0, tiled=True, axis_index_groups=groups)  23.7 us
    all_gather x1, blocking collectives, local(): lax.all_gather(asked, 'ctx', axis=0, tiled=True, axis_index_groups=far)  21 us
    all_to_all x3, starting transfers between devices, a2a(): return lax.all_to_all(x, axis, 0, 0, tiled=True, axis_index_groups=groups)  16.6 us
    pallas_call x1, Pallas kernels, prefix_attention(): pl.pallas_call(attention_kernel, out_shape=jax.ShapeDtypeStruct((groups,...  6.77 us
    all_gather x1, blocking collectives, local(): lax.all_gather(shared, 'ctx', axis=0, tiled=True, axis_index_groups=pairs)  4.37 us
  transfers between devices with their start and end apart: 3, of which 2 were waited for; matrix products, arithmetic and copies ran while one was open for 4% of the time, Pallas kernels for 0%

profile of v7, /device:TPU:1, one launch (start us, length us, event | category | flops | bytes accessed | tf_op | source)
XLA Modules:
  0.0 168.3 jit_solution(7343304545422263987)
XLA Ops:
  0.0 0.9 pad_maximum_fusion
  0.9 15.0 %all_to_all.40 = bf16[8,56,128]{2,1,0:T(8,128)(2,1)S(1)} all-to-all(bf16[8,56,128]{2,1,0:T(8,128)(2,1)S(1)} %pad_maximum_fusion), channel_id=1, replica_groups={{0,1,2,3,4,5,6,7},{8,9,10,11,12,13,14,15},{16,17,18,19,20,21,22,23},{24..., dimensions={0} | all-to-all | bytes 229376 | tf_op jit(solution)/shard_map/split_near/all_to_all | solution.py:135
  16.0 1.2 broadcast_in_dim.41
  17.2 4.8 %all-to-all-start.1 = ((bf16[16,40,1024]{2,1,0:T(8,128)(2,1)}), bf16[16,40,1024]{2,1,0:T(8,128)(2,1)S(1)}, u32[]{:S(2)}, u32[]{:S(2)}) async-start(bf16[16,40,1024]{2,1,0:T(8,128)(2,1)} %broadcast_in_dim.41), calls=%async_computation.1 | async-start | bytes 2621440 | tf_op jit(solution)/shard_map/weights/all_to_all | solution.py:135
  22.3 21.0 %all_gather.6 = bf16[32,16,128]{2,1,0:T(8,128)(2,1)S(1)} all-gather(bf16[8,16,128]{2,1,0:T(8,128)(2,1)S(1)} %slice.44), channel_id=1, replica_groups={{0,8,16,24},{1,9,17,25},{2,10,18,26},{3,11,19,27},{4,12,20,28},{5,13,21..., dimensions={0}, use_global_device_ids=true | all-gather | bytes 163840 | tf_op jit(solution)/shard_map/gather_far/all_gather | solution.py:166
  43.6 11.0 %all_to_all.41 = bf16[8,4,8,128]{3,2,1,0:T(8,128)(2,1)S(1)} all-to-all(bf16[8,4,8,128]{3,2,1,0:T(8,128)(2,1)S(1)} %fusion.1), channel_id=1, replica_groups={{0,1,2,3,4,5,6,7},{8,9,10,11,12,13,14,15},{16,17,18,19,20,21,22,23},{24..., dimensions={0} | all-to-all | bytes 131072 | tf_op jit(solution)/shard_map/slots/all_to_all | solution.py:135
  54.7 1.2 broadcast_in_dim.43
  55.9 7.8 %all-to-all-start.3 = ((bf16[16,256,128]{2,1,0:T(8,128)(2,1)}), bf16[16,256,128]{2,1,0:T(8,128)(2,1)S(1)}, u32[]{:S(2)}, u32[]{:S(2)}) async-start(bf16[16,256,128]{2,1,0:T(8,128)(2,1)} %broadcast_in_dim.43), calls=%async_computation.3 | async-start | bytes 2097152 | tf_op jit(solution)/shard_map/gather_req/all_to_all | solution.py:135
  63.7 3.1 %fusion.34 = (bf16[4,256,512]{2,1,0:T(8,128)(2,1)}, bf16[4,256,512]{2,1,0:T(8,128)(2,1)}) fusion(bf16[4,256,1024]{2,1,0:T(8,128)(2,1)} %param.10), kind=kLoop, calls=%fused_computation.65 | loop fusion | bytes 4194304 | tf_op jit(solution)/shard_map/suffix/slice | solution.py:119
  66.8 12.2 %all-to-all-done.3.q_ref = bf16[16,256,128]{2,1,0:T(8,128)(2,1)S(1)} async-done(((bf16[16,256,128]{2,1,0:T(8,128)(2,1)}), bf16[16,256,128]{2,1,0:T(8,128)(2,1)S(1)}, u32[]{:S(2)}, u32[]{:S(2)}) %all-to-all-start.3) | async-done | bytes 1048608 | tf_op jit(solution)/shard_map/gather_req/all_to_all | solution.py:135
  79.0 6.8 %prefix.1 = bf16[16,272,128]{2,1,0:T(8,128)(2,1)} custom-call(bf16[16,256,128]{2,1,0:T(8,128)(2,1)S(1)} %all-to-all-done.3.q_ref, bf16[1024,1024]{1,0:T(8,128)(2,1)S(1)} %bitcast.71), custom_call_target="tpu_custom_call" | custom-call | flops 2147483648 | bytes 4194304 | tf_op jit(solution)/shard_map/prefix/pallas_call | solution.py:95
  85.8 3.9 %all-to-all-start.4 = ((bf16[16,272,128]{2,1,0:T(8,128)(2,1)}), bf16[16,272,128]{2,1,0:T(8,128)(2,1)S(1)}, u32[]{:S(2)}, u32[]{:S(2)}) async-start(bf16[16,272,128]{2,1,0:T(8,128)(2,1)} %prefix.1), calls=%async_computation.4 | async-start | bytes 2228224 | tf_op jit(solution)/shard_map/prefix/all_to_all | solution.py:135
  89.8 1.6 copy.142
  91.5 0.3 fusion.35
  92.1 0.5 copy.143
  92.6 0.4 fusion.6
  93.2 11.6 %all-to-all-done.4 = bf16[16,272,128]{2,1,0:T(8,128)(2,1)S(1)} async-done(((bf16[16,272,128]{2,1,0:T(8,128)(2,1)}), bf16[16,272,128]{2,1,0:T(8,128)(2,1)S(1)}, u32[]{:S(2)}, u32[]{:S(2)}) %all-to-all-start.4) | async-done | bytes 1114144 | tf_op jit(solution)/shard_map/prefix/all_to_all | solution.py:135
  105.3 0.7 multiply_reduce_fusion
  106.1 26.4 %all_to_all.42 = bf16[32,16,128]{2,1,0:T(8,128)(2,1)S(1)} all-to-all(bf16[32,16,128]{2,1,0:T(8,128)(2,1)S(1)} %maximum_maximum_fusion), channel_id=1, replica_groups=mesh['req'=16,'ctx'=32] {'ctx'}, dimensions={0} | all-to-all | bytes 262144 | tf_op jit(solution)/shard_map/to_heads/all_to_all | solution.py:135
  133.5 7.2 %all_to_all.43 = bf16[4,128,128]{2,1,0:T(8,128)(2,1)S(1)} all-to-all(bf16[4,128,128]{2,1,0:T(8,128)(2,1)S(1)} %broadcast_in_dim.80), channel_id=1, replica_groups={{0,2,4,6},{1,3,5,7},{8,10,12,14},{9,11,13,15},{16,18,20,22},{17,19,21,2..., dimensions={0} | all-to-all | bytes 262144 | tf_op jit(solution)/shard_map/projection/all_to_all | solution.py:135
  140.6 4.4 %all_gather.7 = bf16[8,128,128]{2,1,0:T(8,128)(2,1)S(1)} all-gather(bf16[4,128,128]{2,1,0:T(8,128)(2,1)S(1)} %all_to_all.43), channel_id=1, replica_groups={{0,1},{2,3},{4,5},{6,7},{8,9},{10,11},{12,13},{14,15},{16,17},{18,19},{..., dimensions={0}, use_global_device_ids=true | all-gather | bytes 393216 | tf_op jit(solution)/shard_map/projection/all_gather | solution.py:237
  145.2 0.5 convolution_convert_fusion
  145.8 21.3 %all_to_all.44 = bf16[32,4,640]{2,1,0:T(4,128)(2,1)S(1)} all-to-all(bf16[32,4,640]{2,1,0:T(4,128)(2,1)S(1)} %reshape.212), channel_id=1, replica_groups=mesh['req'=16,'ctx'=32] {'ctx'}, dimensions={0} | all-to-all | bytes 327680 | tf_op jit(solution)/shard_map/projection/all_to_all | solution.py:135
  167.5 0.8 reshape.215
  (68 shorter events, 3.2 us)
Async XLA Ops:
  17.2 4.9 %copy-start.5 = (s32[128]{0:T(128)S(1)}, s32[128]{0:T(128)}, u32[]{:S(2)}) copy-start(s32[128]{0:T(128)} %param.7) | copy-start | bytes 1540
  17.2 26.4 %all-to-all-start.1 = ((bf16[16,40,1024]{2,1,0:T(8,128)(2,1)}), bf16[16,40,1024]{2,1,0:T(8,128)(2,1)S(1)}, u32[]{:S(2)}, u32[]{:S(2)}) async-start(bf16[16,40,1024]{2,1,0:T(8,128)(2,1)} %broadcast_in_dim.41), calls=%async_computation.1 | async-start | bytes 2621440 | tf_op jit(solution)/shard_map/weights/all_to_all | solution.py:135
  43.6 12.2 %copy-start.1 = (bf16[16,40,1024]{2,1,0:T(8,128)(2,1)}, bf16[16,40,1024]{2,1,0:T(8,128)(2,1)S(1)}, u32[]{:S(2)}) copy-start(bf16[16,40,1024]{2,1,0:T(8,128)(2,1)S(1)} %all-to-all-done.1) | copy-start | bytes 3932164
  55.9 23.2 %all-to-all-start.3 = ((bf16[16,256,128]{2,1,0:T(8,128)(2,1)}), bf16[16,256,128]{2,1,0:T(8,128)(2,1)S(1)}, u32[]{:S(2)}, u32[]{:S(2)}) async-start(bf16[16,256,128]{2,1,0:T(8,128)(2,1)} %broadcast_in_dim.43), calls=%async_computation.3 | async-start | bytes 2097152 | tf_op jit(solution)/shard_map/gather_req/all_to_all | solution.py:135
  63.7 15.3 %copy-start = (bf16[1,1024,1024]{2,1,0:T(8,128)(2,1)S(1)}, bf16[1,1024,1024]{2,1,0:T(8,128)(2,1)}, u32[]{:S(2)}) copy-start(bf16[1,1024,1024]{2,1,0:T(8,128)(2,1)} %param.9) | copy-start | bytes 6291460
  85.8 4.0 %copy-start.6 = (s32[1,4]{1,0:T(1,128)S(1)}, s32[1,4]{1,0:T(1,128)}, u32[]{:S(2)}) copy-start(s32[1,4]{1,0:T(1,128)} %param.8) | copy-start | bytes 52
  85.8 18.9 %all-to-all-start.4 = ((bf16[16,272,128]{2,1,0:T(8,128)(2,1)}), bf16[16,272,128]{2,1,0:T(8,128)(2,1)S(1)}, u32[]{:S(2)}, u32[]{:S(2)}) async-start(bf16[16,272,128]{2,1,0:T(8,128)(2,1)} %prefix.1), calls=%async_computation.4 | async-start | bytes 2228224 | tf_op jit(solution)/shard_map/prefix/all_to_all | solution.py:135
  89.8 1.7 copy-start.4
  89.8 2.3 %copy-start.3 = (bf16[4,256,512]{2,1,0:T(8,128)(2,1)S(1)}, bf16[4,256,512]{2,1,0:T(8,128)(2,1)}, u32[]{:S(2)}) copy-start(bf16[4,256,512]{2,1,0:T(8,128)(2,1)} %get-tuple-element.12) | copy-start | bytes 3145732
  106.0 39.2 %copy-start.2 = (bf16[16,40,1024]{2,1,0:T(8,128)(2,1)S(1)}, bf16[16,40,1024]{2,1,0:T(8,128)(2,1)}, u32[]{:S(2)}) copy-start(bf16[16,40,1024]{2,1,0:T(8,128)(2,1)} %copy-done.1) | copy-start | bytes 3932164
